TPU v7x, 128 devices: a whole 4x4x4 slice. The times are simulated.
128 devices in a mesh: rep: 4 (over z), tile: 32 (over y, x, core).
Axes of the slice: x: 4, y: 4, z: 4, core: 2. Of those that a mesh axis runs over, the one named last changes fastest.
Arguments:
- features: bfloat16 [512, 32, 32, 256], P(('rep', 'tile')), may hold values from -6 to 6
- cotangent: bfloat16 [512, 32, 2048], P(('rep', 'tile')), may hold values from -0.29882812 to 0.29882812
- neighbors: int32 [512, 8], P(('rep', 'tile')), may hold values from -1 to 3, as said below
- live_count: int32 [128], P(('rep', 'tile')), may hold values from 1 to 4, as said below
- kernel_mid: bfloat16 [3, 3, 256, 128], replicated, may hold values from -0.125 to 0.125
- bias_mid: float32 [128], replicated, may hold values from -0.5 to 0.5
- kernel_top: bfloat16 [3, 3, 128, 64], replicated, may hold values from -0.1875 to 0.1875
- bias_top: float32 [64], replicated, may hold values from -0.5 to 0.5
Outputs:
- backend_out: bfloat16 [512, 32, 2048], P(('rep', 'tile'))
- gradient_mid: float32 [3, 3, 256, 128], replicated
- gradbias_mid: float32 [128], replicated
- gradient_top: float32 [3, 3, 128, 64], replicated
- gradbias_top: float32 [64], replicated
Inputs may be any that keep to these rules, and one draw needn't show every extreme that they name: Slots 0 to live_count - 1 of a column hold populated tiles; some column holds 4 in every draw. `neighbors`: entry k names a live slot of the column offset by that direction's dc within the same scene, whose tile sits at the adjacent scene position; -1 where no populated tile is there, for every direction of an empty slot, and past either end of a scene's 32 columns. Two live slots of one column never sit at the same position.
All inputs are finite; a program needn't handle non-finite values.
Results may differ from a plain program's by a relative error of at most 0.009.
Values may be sent and summed in bfloat16 or wider, within the bound.
A program may use at most 128 MiB of HBM per device.

v0:
```python
import functools

import jax
import jax.numpy as jnp
from jax import lax
from jax.experimental import pallas as pl
from jax.experimental.pallas import tpu as pltpu
from jax.sharding import PartitionSpec as P

F32 = jnp.float32
BF16 = jnp.bfloat16
MESH = pl.DeviceIdType.MESH

SLOTS = 4
SIDE = 32
CELLS = SIDE * SIDE
PADDED = CELLS + 128
WIDE = 40
FULL = 48


def sigmoid(v):
    return 0.5 * jnp.tanh(0.5 * v) + 0.5


def low_lanes(shape):
    return lax.broadcasted_iota(jnp.int32, shape, len(shape) - 1) < 64


def present(index):
    return jnp.where(index >= 0, 1.0, 0.0).astype(F32)


def fill_bands(padded, nbr):
    for t in range(SLOTS):
        north, south = nbr[t, 1], nbr[t, 6]
        band = padded[jnp.maximum(north, 0), CELLS : CELLS + 64, :].astype(F32)
        padded[t, 0:64, :] = (band * present(north)).astype(BF16)
        band = padded[jnp.maximum(south, 0), 64:128, :].astype(F32)
        padded[t, CELLS + 64 : PADDED, :] = (band * present(south)).astype(BF16)


def strip_block(received, index, col, lanes):
    return received[jnp.maximum(index, 0) * 2 + col, :, lanes].astype(F32) * present(index)


def margin_strips(received, nbr, corner_up, side, corner_down, work, shifted, channels):
    for lane_tile in range(channels // 128):
        lanes = slice(lane_tile * 128, lane_tile * 128 + 128)
        for t in range(SLOTS):
            for col in range(2):
                base = (t * 2 + col) * FULL
                up = strip_block(received, nbr[t, corner_up], col, lanes)
                mid = strip_block(received, nbr[t, side], col, lanes)
                down = strip_block(received, nbr[t, corner_down], col, lanes)
                work[base : base + 8, :] = up[24:32]
                work[base + 8 : base + 40, :] = mid
                work[base + 40 : base + 48, :] = down[0:8]
        for block in range(SLOTS * 2):
            for a in range(3):
                rows = work[block * FULL + 6 + 2 * a : block * FULL + 38 + 2 * a, :]
                at = a * channels + lane_tile * 128
                shifted[block * 32 : block * 32 + 32, at : at + 128] = rows.astype(BF16)


def kernel(
    feat, cot, nbr, live, kmid, bmid, ktop, btop,
    out, grad,
    fp, hp, wmid, wtop, wback, y0, y1, y2, ya, yb, work, sa_w, sa_e, sh_w, sh_e, su_w, su_e,
    strip_a, strip_b, fsend, frecv, hsend, hrecv, usend, urecv,
    slope, cots, outs, uf, uplo, uphi, uu, ucol_w, ucol_e, scol_w, scol_e, sf, ss,
    acc_mid, acc_top, cotv,
    local_sem, send_sem, recv_sem,
):
    n = lax.axis_size("tile")
    me = lax.axis_index("tile")
    right, left = lax.rem(me + 1, n), lax.rem(me + n - 1, n)

    loads = []
    for t in range(SLOTS):
        loads.append(pltpu.make_async_copy(
            feat.at[t], fp.at[t, pl.ds(64, CELLS)], local_sem.at[t]))
    for a in range(3):
        for b in range(3):
            loads.append(pltpu.make_async_copy(
                kmid.at[a, b],
                wmid.at[pl.ds(a * 256, 256), pl.ds(b * 128, 128)],
                local_sem.at[4 + a * 3 + b]))
    loads.append(pltpu.make_async_copy(cot, cotv, local_sem.at[13]))
    for copy in loads:
        copy.start()

    barrier = pltpu.get_barrier_semaphore()
    for neighbour in (left, right):
        pl.semaphore_signal(barrier, inc=1, device_id={"tile": neighbour}, device_id_type=MESH)

    zero8 = jnp.zeros((8, 128), F32)

    def clear(r, _):
        base = pl.multiple_of(r * FULL, 8)
        uf[pl.ds(base, 8), :] = zero8
        uf[pl.ds(base + 40, 8), :] = zero8
        sf[pl.ds(base, 8), :] = zero8
        sf[pl.ds(base + 40, 8), :] = zero8
        return 0

    lax.fori_loop(0, SLOTS * SIDE, clear, 0)

    for a in range(3):
        k0, k1, k2 = (ktop[a, b] for b in range(3))
        wtop[a * 128 : a * 128 + 128, 0:128] = jnp.concatenate([k0, k2], axis=1)
        wtop[a * 128 : a * 128 + 128, 128:256] = jnp.concatenate([k1, k1], axis=1)
    zero_kernel = jnp.zeros((128, 64), F32)
    for b in range(3):
        first = jnp.concatenate([ktop[2, 2 - b], ktop[1, 2 - b]], axis=1).astype(F32)
        last = jnp.concatenate([ktop[0, 2 - b].astype(F32), zero_kernel], axis=1)
        wback[0:128, b * 128 : b * 128 + 128] = first.T.astype(BF16)
        wback[128:256, b * 128 : b * 128 + 128] = last.T.astype(BF16)

    for copy in loads[:SLOTS]:
        copy.wait()

    for side, (cells, picks) in enumerate(((0, (0, 1)), (16, (6, 7)))):
        def gather(r, _):
            t, i = r // SIDE, r % SIDE
            rows = fp[t, pl.ds(pl.multiple_of(64 + i * SIDE + cells, 16), 16), :].astype(F32)
            rows = rows[0:8] if cells == 0 else rows[8:16]
            at = pl.multiple_of(r * 8, 8)
            strip_a[pl.ds(at, 8), :] = rows[:, 0:128]
            strip_b[pl.ds(at, 8), :] = rows[:, 128:256]
            return 0

        lax.fori_loop(0, SLOTS * SIDE, gather, 0, unroll=4)
        for t in range(SLOTS):
            for col, pick in enumerate(picks):
                at = pl.ds(t * 256 + pick, 32, stride=8)
                fsend[side, t * 2 + col, :, 0:128] = strip_a[at, :].astype(BF16)
                fsend[side, t * 2 + col, :, 128:256] = strip_b[at, :].astype(BF16)

    pl.semaphore_wait(barrier, 2)

    def exchange(send, recv, at):
        copies = []
        for side, target in ((0, left), (1, right)):
            copies.append(pltpu.make_async_remote_copy(
                src_ref=send.at[side], dst_ref=recv.at[1 - side],
                send_sem=send_sem.at[at + side], recv_sem=recv_sem.at[at + 1 - side],
                device_id={"tile": target}, device_id_type=MESH))
        for copy in copies:
            copy.start()
        return copies

    feature_copies = exchange(fsend, frecv, 0)

    fill_bands(fp, nbr)
    for copy in loads[SLOTS:]:
        copy.wait()

    def conv_mid(t, _):
        lhs = jnp.concatenate([fp[t, 64 * a : 64 * a + CELLS, :] for a in range(3)], axis=1)
        y = jnp.dot(lhs, wmid[...], preferred_element_type=F32)
        for i in range(SIDE):
            r = t * SIDE + i
            rows = slice(i * SIDE, i * SIDE + SIDE)
            y0[pl.ds(pl.multiple_of(r * WIDE + 8, 8), SIDE), :] = y[rows, 0:128]
            y1[pl.ds(pl.multiple_of(r * SIDE, 8), SIDE), :] = y[rows, 128:256]
            y2[pl.ds(pl.multiple_of(r * WIDE, 8), SIDE), :] = y[rows, 256:384]
        return 0

    lax.fori_loop(0, SLOTS, conv_mid, 0)

    low = low_lanes((SIDE, 128))
    for t in range(SLOTS):
        for pair in range(SIDE // 2):
            x = cotv[t, :, pair * 128 : pair * 128 + 128].astype(F32)
            turned = pltpu.roll(x, 64, 1)
            cots[pl.ds(t * CELLS + 2 * pair, SIDE, stride=SIDE), :] = jnp.where(low, x, turned)
            cots[pl.ds(t * CELLS + 2 * pair + 1, SIDE, stride=SIDE), :] = jnp.where(low, turned, x)

    for copy in feature_copies:
        copy.wait()
    margin_strips(frecv.at[0], nbr, 0, 3, 5, work, sa_w, 256)
    margin_strips(frecv.at[1], nbr, 2, 4, 7, work, sa_e, 256)

    def add_margins(west, east):
        for t in range(SLOTS):
            for col in range(2):
                rows = slice((t * 2 + col) * 32, (t * 2 + col) * 32 + 32)
                y0[pl.ds(t * SIDE * WIDE + 6 + col, SIDE, stride=WIDE), :] = west[rows]
                y2[pl.ds(t * SIDE * WIDE + 32 + col, SIDE, stride=WIDE), :] = east[rows]

    add_margins(
        jnp.dot(sa_w[...], wmid[:, 0:128], preferred_element_type=F32),
        jnp.dot(sa_e[...], wmid[:, 256:384], preferred_element_type=F32))

    alive = [jnp.where(t < live[0], 1.0, 0.0).astype(F32) for t in range(SLOTS)]
    columns = ((0, 0, 0), (0, 1, 1), (1, 0, 30), (1, 1, 31))

    def mid_at(t, cell):
        first = y0[pl.ds(t * SIDE * WIDE + 6 + cell, SIDE, stride=WIDE), :]
        second = y1[pl.ds(t * CELLS + cell, SIDE, stride=SIDE), :]
        third = y2[pl.ds(t * SIDE * WIDE + 2 + cell, SIDE, stride=WIDE), :]
        return first + second + third

    for t in range(SLOTS):
        for side, col, cell in columns:
            pre = mid_at(t, cell) + bmid[...]
            hsend[side, t * 2 + col, :, :] = (pre * sigmoid(pre) * alive[t]).astype(BF16)
    hidden_copies = exchange(hsend, hrecv, 2)

    def mid_rows(r):
        first = y0[pl.ds(r * WIDE + 6, SIDE), :]
        second = y1[pl.ds(pl.multiple_of(r * SIDE, 8), SIDE), :]
        third = y2[pl.ds(r * WIDE + 2, SIDE), :]
        return first + second + third

    def activate(r, _):
        t, i = r // SIDE, r % SIDE
        mask = jnp.where(t < live[0], 1.0, 0.0).astype(F32)
        pre = mid_rows(r) + bmid[...]
        gate = sigmoid(pre)
        hidden = pre * gate
        hp[t, pl.ds(pl.multiple_of(64 + i * SIDE, 16), SIDE), :] = (hidden * mask).astype(BF16)
        slope[pl.ds(pl.multiple_of(r * SIDE, 8), SIDE), :] = (gate + hidden * (1.0 - gate)) * mask
        return 0

    lax.fori_loop(0, SLOTS * SIDE, activate, 0, unroll=4)
    fill_bands(hp, nbr)

    def conv_top(t, _):
        lhs = jnp.concatenate([hp[t, 64 * a : 64 * a + CELLS, :] for a in range(3)], axis=1)
        y = jnp.dot(lhs, wtop[...], preferred_element_type=F32)
        for i in range(SIDE):
            r = t * SIDE + i
            rows = slice(i * SIDE, i * SIDE + SIDE)
            ya[pl.ds(pl.multiple_of(r * FULL + 8, 8), SIDE), :] = y[rows, 0:128]
            yb[pl.ds(pl.multiple_of(r * SIDE, 8), SIDE), :] = y[rows, 128:256]
        return 0

    lax.fori_loop(0, SLOTS, conv_top, 0)

    for copy in hidden_copies:
        copy.wait()
    margin_strips(hrecv.at[0], nbr, 0, 3, 5, work, sh_w, 128)
    margin_strips(hrecv.at[1], nbr, 2, 4, 7, work, sh_e, 128)
    west = jnp.dot(sh_w[...], wtop[:, 0:128], preferred_element_type=F32)
    east = jnp.dot(sh_e[...], wtop[:, 0:128], preferred_element_type=F32)
    for t in range(SLOTS):
        for col in range(2):
            rows = slice((t * 2 + col) * 32, (t * 2 + col) * 32 + 32)
            ya[pl.ds(t * SIDE * FULL + 6 + col, SIDE, stride=FULL), :] = west[rows]
            ya[pl.ds(t * SIDE * FULL + 40 + col, SIDE, stride=FULL), :] = east[rows]

    def up_of(before, after, centre, cotangent):
        pair = jnp.where(low, before, after)
        pre = pair + pltpu.roll(pair, 64, 1) + centre + btop[...]
        gate = sigmoid(pre)
        value = pre * gate
        return value, cotangent * (gate + value * (1.0 - gate))

    zero_rows = jnp.zeros((SIDE, 128), F32)
    for t in range(SLOTS):
        for side in range(2):
            ups = []
            for col in range(2):
                cell = 30 * side + col
                _, up = up_of(
                    ya[pl.ds(t * SIDE * FULL + 6 + cell, SIDE, stride=FULL), :],
                    ya[pl.ds(t * SIDE * FULL + 10 + cell, SIDE, stride=FULL), :],
                    yb[pl.ds(t * CELLS + cell, SIDE, stride=SIDE), :],
                    cots[pl.ds(t * CELLS + cell, SIDE, stride=SIDE), :])
                up = up * alive[t]
                ups.append(up)
                edge = ucol_w if side == 0 else ucol_e
                at = (t * 2 + col) * 32
                edge[at : at + 32, :] = jnp.where(low, up, zero_rows).astype(BF16)
            usend[side, t] = jnp.where(low, ups[0], ups[1]).astype(BF16)
    upstream_copies = exchange(usend, urecv, 4)

    def top_rows(r, total):
        t, i = r // SIDE, r % SIDE
        mask = jnp.where(t < live[0], 1.0, 0.0).astype(F32)
        value, up = up_of(
            ya[pl.ds(r * FULL + 6, SIDE), :],
            ya[pl.ds(r * FULL + 10, SIDE), :],
            yb[pl.ds(pl.multiple_of(r * SIDE, 8), SIDE), :],
            cots[pl.ds(pl.multiple_of(r * SIDE, 8), SIDE), :])
        outs[pl.ds(pl.multiple_of(r * SIDE, 8), SIDE), :] = value * mask
        up = (up * mask).astype(BF16).astype(F32)
        uf[pl.ds(pl.multiple_of(r * FULL + 8, 8), SIDE), :] = up
        at = pl.ds(pl.multiple_of(64 + i * SIDE, 16), SIDE)
        uplo[t, at, :] = jnp.where(low, up, zero_rows).astype(BF16)
        uphi[t, at, :] = jnp.where(low, zero_rows, up).astype(BF16)
        return total + jnp.sum(up.reshape(4, 8, 128), axis=0)

    bias_top = lax.fori_loop(0, SLOTS * SIDE, top_rows, jnp.zeros((8, 128), F32), unroll=4)
    fill_bands(uplo, nbr)
    fill_bands(uphi, nbr)

    def shift_up(r, _):
        before = uf[pl.ds(r * FULL + 6, SIDE), :]
        same = uf[pl.ds(pl.multiple_of(r * FULL + 8, 8), SIDE), :]
        after = uf[pl.ds(r * FULL + 10, SIDE), :]
        at = pl.ds(pl.multiple_of(r * SIDE, 16), SIDE)
        uu[at, 0:128] = jnp.where(low, after, same).astype(BF16)
        uu[at, 128:256] = before.astype(BF16)
        return 0

    lax.fori_loop(0, SLOTS * SIDE, shift_up, 0, unroll=4)

    for t in range(SLOTS):
        for pair in range(SIDE // 2):
            x0 = outs[pl.ds(t * CELLS + 2 * pair, SIDE, stride=SIDE), :]
            x1 = outs[pl.ds(t * CELLS + 2 * pair + 1, SIDE, stride=SIDE), :]
            out[t, :, pair * 128 : pair * 128 + 128] = jnp.where(low, x0, x1).astype(BF16)

    zero_cols = jnp.zeros((256, 128), BF16)
    edges_l = jnp.concatenate([
        jnp.concatenate([ucol_w[...], zero_cols], axis=1),
        jnp.concatenate([zero_cols, ucol_e[...]], axis=1)], axis=0)
    edges_r = jnp.concatenate([sh_w[...], sh_e[...]], axis=0)
    across = (((0,), (0,)), ((), ()))
    acc_top[...] = lax.dot_general(edges_l, edges_r, across, preferred_element_type=F32)

    def grad_top(t, _):
        rhs = jnp.concatenate([hp[t, 64 * a : 64 * a + CELLS, :] for a in range(3)], axis=1)
        lhs = uu[pl.ds(pl.multiple_of(t * CELLS, 16), CELLS), :]
        acc_top[...] += lax.dot_general(lhs, rhs, across, preferred_element_type=F32)
        return 0

    lax.fori_loop(0, SLOTS, grad_top, 0)

    def conv_back(t, _):
        first = uplo[t, 0:CELLS, :] + uphi[t, 64 : 64 + CELLS, :]
        lhs = jnp.concatenate([first, uplo[t, 128 : 128 + CELLS, :]], axis=1)
        y = jnp.dot(lhs, wback[...], preferred_element_type=F32)
        for i in range(SIDE):
            r = t * SIDE + i
            rows = slice(i * SIDE, i * SIDE + SIDE)
            y0[pl.ds(pl.multiple_of(r * WIDE + 8, 8), SIDE), :] = y[rows, 0:128]
            y1[pl.ds(pl.multiple_of(r * SIDE, 8), SIDE), :] = y[rows, 128:256]
            y2[pl.ds(pl.multiple_of(r * WIDE, 8), SIDE), :] = y[rows, 256:384]
        return 0

    lax.fori_loop(0, SLOTS, conv_back, 0)

    for copy in upstream_copies:
        copy.wait()
    for received, up, side, down, dest in (
        (urecv.at[0], 0, 3, 5, su_w), (urecv.at[1], 2, 4, 7, su_e)):
        def strip_of(index):
            return received[jnp.maximum(index, 0)].astype(F32) * present(index)

        for t in range(SLOTS):
            base = t * FULL
            work[base : base + 8, :] = strip_of(nbr[t, up])[24:32]
            work[base + 8 : base + 40, :] = strip_of(nbr[t, side])
            work[base + 40 : base + 48, :] = strip_of(nbr[t, down])[0:8]
        for t in range(SLOTS):
            v = [work[t * FULL + 6 + 2 * a : t * FULL + 38 + 2 * a, :] for a in range(3)]
            w = [pltpu.roll(x, 64, 1) for x in v]
            at = t * 64
            dest[at : at + 32, 0:128] = jnp.where(low, v[0], w[1]).astype(BF16)
            dest[at : at + 32, 128:256] = jnp.where(low, v[2], zero_rows).astype(BF16)
            dest[at + 32 : at + 64, 0:128] = jnp.where(low, w[0], v[1]).astype(BF16)
            dest[at + 32 : at + 64, 128:256] = jnp.where(low, w[2], zero_rows).astype(BF16)
    add_margins(
        jnp.dot(su_w[...], wback[:, 0:128], preferred_element_type=F32),
        jnp.dot(su_e[...], wback[:, 256:384], preferred_element_type=F32))

    def slopes(r, total):
        back = mid_rows(r) * slope[pl.ds(pl.multiple_of(r * SIDE, 8), SIDE), :]
        back = back.astype(BF16).astype(F32)
        sf[pl.ds(pl.multiple_of(r * FULL + 8, 8), SIDE), :] = back
        return total + jnp.sum(back.reshape(4, 8, 128), axis=0)

    bias_mid = lax.fori_loop(0, SLOTS * SIDE, slopes, jnp.zeros((8, 128), F32), unroll=4)

    def shift_slope(r, _):
        at = pl.ds(pl.multiple_of(r * SIDE, 16), SIDE)
        ss[at, 0:128] = sf[pl.ds(r * FULL + 10, SIDE), :].astype(BF16)
        ss[at, 128:256] = sf[pl.ds(pl.multiple_of(r * FULL + 8, 8), SIDE), :].astype(BF16)
        ss[at, 256:384] = sf[pl.ds(r * FULL + 6, SIDE), :].astype(BF16)
        return 0

    lax.fori_loop(0, SLOTS * SIDE, shift_slope, 0, unroll=4)
    for t in range(SLOTS):
        for side, col, cell in columns:
            edge = scol_w if side == 0 else scol_e
            at = (t * 2 + col) * 32
            edge[at : at + 32, :] = sf[
                pl.ds(t * SIDE * FULL + 8 + cell, SIDE, stride=FULL), :].astype(BF16)

    acc_mid[0:128, :] = lax.dot_general(scol_w[...], sa_w[...], across, preferred_element_type=F32)
    acc_mid[128:256, :] = jnp.zeros((128, 768), F32)
    acc_mid[256:384, :] = lax.dot_general(scol_e[...], sa_e[...], across, preferred_element_type=F32)

    def grad_mid(t, _):
        rhs = jnp.concatenate([fp[t, 64 * a : 64 * a + CELLS, :] for a in range(3)], axis=1)
        lhs = ss[pl.ds(pl.multiple_of(t * CELLS, 16), CELLS), :]
        acc_mid[...] += lax.dot_general(lhs, rhs, across, preferred_element_type=F32)
        return 0

    lax.fori_loop(0, SLOTS, grad_mid, 0)

    for a in range(3):
        for b in range(3):
            at = (a * 3 + b) * 256
            grad[at : at + 256, :] = acc_mid[b * 128 : b * 128 + 128, a * 256 : a * 256 + 256].T
        for half in range(2):
            at = 2304 + half * 384 + a * 128
            grad[at : at + 128, :] = acc_top[
                half * 128 : half * 128 + 128, a * 128 : a * 128 + 128].T
    grad[3072:3080, :] = bias_mid
    grad[3080:3088, :] = bias_top


def shards(features, cotangent, neighbors, live_count, kernel_mid, bias_mid, kernel_top, bias_top):
    slots, side, _, channels = features.shape
    vmem = pl.BlockSpec(memory_space=pltpu.VMEM)
    smem = pl.BlockSpec(memory_space=pltpu.SMEM)
    hbm = pl.BlockSpec(memory_space=pl.ANY)
    rows = SLOTS * SIDE
    out, grad = pl.pallas_call(
        kernel,
        out_shape=(
            jax.ShapeDtypeStruct((SLOTS, SIDE, 2048), BF16),
            jax.ShapeDtypeStruct((3088, 128), F32),
        ),
        in_specs=[hbm, hbm, smem, smem, hbm, vmem, vmem, vmem],
        out_specs=(vmem, vmem),
        scratch_shapes=[
            pltpu.VMEM((SLOTS, PADDED, 256), BF16),
            pltpu.VMEM((SLOTS, PADDED, 128), BF16),
            pltpu.VMEM((768, 384), BF16),
            pltpu.VMEM((384, 256), BF16),
            pltpu.VMEM((256, 384), BF16),
            pltpu.VMEM((rows * WIDE, 128), F32),
            pltpu.VMEM((rows * SIDE, 128), F32),
            pltpu.VMEM((rows * WIDE, 128), F32),
            pltpu.VMEM((rows * FULL, 128), F32),
            pltpu.VMEM((rows * SIDE, 128), F32),
            pltpu.VMEM((8 * FULL, 128), F32),
            pltpu.VMEM((256, 768), BF16),
            pltpu.VMEM((256, 768), BF16),
            pltpu.VMEM((256, 384), BF16),
            pltpu.VMEM((256, 384), BF16),
            pltpu.VMEM((256, 256), BF16),
            pltpu.VMEM((256, 256), BF16),
            pltpu.VMEM((rows * 8, 128), F32),
            pltpu.VMEM((rows * 8, 128), F32),
            pltpu.VMEM((2, 8, 32, 256), BF16),
            pltpu.VMEM((2, 8, 32, 256), BF16),
            pltpu.VMEM((2, 8, 32, 128), BF16),
            pltpu.VMEM((2, 8, 32, 128), BF16),
            pltpu.VMEM((2, 4, 32, 128), BF16),
            pltpu.VMEM((2, 4, 32, 128), BF16),
            pltpu.VMEM((rows * SIDE, 128), F32),
            pltpu.VMEM((rows * SIDE, 128), F32),
            pltpu.VMEM((rows * SIDE, 128), F32),
            pltpu.VMEM((rows * FULL, 128), F32),
            pltpu.VMEM((SLOTS, PADDED, 128), BF16),
            pltpu.VMEM((SLOTS, PADDED, 128), BF16),
            pltpu.VMEM((rows * SIDE, 256), BF16),
            pltpu.VMEM((256, 128), BF16),
            pltpu.VMEM((256, 128), BF16),
            pltpu.VMEM((256, 128), BF16),
            pltpu.VMEM((256, 128), BF16),
            pltpu.VMEM((rows * FULL, 128), F32),
            pltpu.VMEM((rows * SIDE, 384), BF16),
            pltpu.VMEM((384, 768), F32),
            pltpu.VMEM((256, 384), F32),
            pltpu.VMEM((SLOTS, SIDE, 2048), BF16),
            pltpu.SemaphoreType.DMA((14,)),
            pltpu.SemaphoreType.DMA((6,)),
            pltpu.SemaphoreType.DMA((6,)),
        ],
        compiler_params=pltpu.CompilerParams(
            collective_id=0, has_side_effects=True, vmem_limit_bytes=60 * 2**20),
        name="backend_layers",
    )(
        features.reshape(slots, side * side, channels), cotangent, neighbors, live_count,
        kernel_mid, bias_mid.reshape(1, 128), kernel_top,
        jnp.concatenate([bias_top, bias_top]).reshape(1, 128),
    )
    grad = lax.psum(grad, ("rep", "tile"))
    grad_mid = grad[:2304].reshape(3, 3, 256, 128)
    low = grad[2304:2688].reshape(3, 128, 2, 64).transpose(0, 2, 1, 3)
    high = grad[2688:3072, 0:64].reshape(3, 1, 128, 64)
    grad_top = jnp.concatenate([low, high], axis=1)
    bias_mid_sum = jnp.sum(grad[3072:3080], axis=0)
    bias_top_sum = jnp.sum(grad[3080:3088, 0:64], axis=0)
    return out, grad_mid, bias_mid_sum, grad_top, bias_top_sum


def solution(mesh):
    in_specs = (
        P(("rep", "tile"), None, None, None),
        P(("rep", "tile"), None, None),
        P(("rep", "tile"), None),
        P(("rep", "tile")),
        P(),
        P(),
        P(),
        P(),
    )
    out_specs = (P(("rep", "tile"), None, None), P(), P(), P(), P())
    return jax.shard_map(shards, mesh=mesh, in_specs=in_specs, out_specs=out_specs, check_vma=False)
```

profile of v0, /device:TPU:1, one launch (start us, length us, event | category | flops | bytes accessed | tf_op | source)
XLA Modules:
  0.0 208.8 jit_solution(17009470678102875270)
XLA Ops:
  7.2 0.0 all-reduce.2.cloned.1.call-start
  7.9 1.3 maximum_bitcast_fusion.btop
  9.2 1.8 copy.16.ktop
  11.0 33.2 %backend_layers.1 = (bf16[4,32,2048]{2,1,0:T(8,128)(2,1)}, f32[3088,128]{1,0:T(8,128)}) custom-call(bf16[4,1024,256]{2,1,0:T(8,128)(2,1)} %bitcast.9, bf16[4,32,2048]{2,1,0:T(8,128)(2,1)} %cot.1, s32[4,8]{1,0:T(4,128)} %nbr.1, s32[1]{0:T(128)S(6)} %copy.22.live, bf16[3,3,256,128]{3,2,1,0:T(8,128)(2,1)} %kmid.1, f32[1,128]{1,0:T(1,128)} %bitcast.13, ...), custom_call_target="tpu_custom_call" | custom-call | tf_op jit(solution)/shard_map/backend_layers/pallas_call | solution.py:424
  44.2 0.0 all-reduce.2.cloned.1.call-update
  44.2 151.6 %all-reduce.2.cloned.1.call-done = f32[3088,128]{1,0:T(8,128)} async-done(((f32[3088,128]{1,0:T(8,128)}), f32[3088,128]{1,0:T(8,128)}) %all-reduce.2.cloned.1.call-update) | async-done | bytes 1581072 | tf_op jit(solution)/shard_map/psum | solution.py:486
  195.8 0.9 slice.23
  196.8 0.0 copy-start
  196.8 0.1 copy.18
  196.9 1.0 slice.22
  198.0 0.1 copy.17
  198.1 0.1 reshape.32
  198.2 0.1 pad_maximum_fusion
  198.3 0.0 copy-start.1
  198.3 0.7 copy.19
  199.0 0.0 copy-done
  199.0 0.5 slice_reduce_fusion
  199.6 0.5 slice_reduce_fusion.1
  200.1 1.1 slice.20
  201.2 0.0 copy-done.1
  201.2 0.8 copy.23
Async XLA Ops:
  7.2 188.7 %all-reduce.2.cloned.1.call-start = ((), (), s32[]{:S(2)}) async-start(), calls=%async_computation | async-start | bytes 3162112 | tf_op jit(solution)/shard_map/psum | solution.py:486
  196.8 2.3 %copy-start = (f32[3088,128]{1,0:T(8,128)S(1)}, f32[3088,128]{1,0:T(8,128)}, u32[]{:S(2)}) copy-start(f32[3088,128]{1,0:T(8,128)} %all-reduce.2.cloned.1.call-done) | copy-start | bytes 4743172
  198.3 2.9 %copy-start.1 = (bf16[4,32,2048]{2,1,0:T(8,128)(2,1)S(1)}, bf16[4,32,2048]{2,1,0:T(8,128)(2,1)}, u32[]{:S(2)}) copy-start(bf16[4,32,2048]{2,1,0:T(8,128)(2,1)} %get-tuple-element.19) | copy-start | bytes 1572868
Sparse Core Ops, SparseCore 0:
  44.4 151.4 all-reduce.1
where the time goes:
time: 209 us
  waiting for transfers between devices  152 us (73%)
  Pallas kernels  33.2 us (16%)
  between operations  14.7 us (7%)
  local copies, waits for them, and re-layouts  6.73 us (3%)
  other arithmetic  2.46 us (1%)
    psum x1, waiting for transfers between devices, shards(): grad = lax.psum(grad, ('rep', 'tile'))  152 us
    pallas_call x1, Pallas kernels, shards(): pl.pallas_call(kernel, out_shape=(jax.ShapeDtypeStruct((SLOTS, SIDE, 2048...  33.2 us
  transfers between devices with their start and end apart: 1, of which 1 were waited for; matrix products, arithmetic and copies ran while one was open for 0% of the time, Pallas kernels for 0%

commit v1 on v0

--- a/solution.py
+++ b/solution.py
@@ -65,16 +65,27 @@
 
 def kernel(
     feat, cot, nbr, live, kmid, bmid, ktop, btop,
-    out, grad,
+    out, gmid_out, gtop_out, bmid_out, btop_out,
     fp, hp, wmid, wtop, wback, y0, y1, y2, ya, yb, work, sa_w, sa_e, sh_w, sh_e, su_w, su_e,
     strip_a, strip_b, fsend, frecv, hsend, hrecv, usend, urecv,
-    slope, cots, outs, uf, uplo, uphi, uu, ucol_w, ucol_e, scol_w, scol_e, sf, ss,
-    acc_mid, acc_top, cotv,
-    local_sem, send_sem, recv_sem,
+    slope, cots, outs, uf, uplo, uphi, uu, ucol_w, ucol_e, scol_w, scol_e, sf,
+    sst, acc_top, cotv, grad, sum_core, core_in, first_out, first_in, second_out, second_in,
+    third_in, second_back, first_back, total,
+    local_sem, send_sem, recv_sem, sum_send, sum_recv,
 ):
     n = lax.axis_size("tile")
     me = lax.axis_index("tile")
     right, left = lax.rem(me + 1, n), lax.rem(me + n - 1, n)
+    z, y, x, core = lax.axis_index("rep"), me // 8, lax.rem(me // 2, 4), lax.rem(me, 2)
+    place = {"x": x, "y": y, "z": z}
+
+    def on_chip(where, c):
+        return {"rep": where["z"], "tile": where["y"] * 8 + where["x"] * 2 + c}
+
+    def along(axis, distance):
+        there = dict(place)
+        there[axis] = lax.rem(place[axis] + distance, 4)
+        return on_chip(there, core)
 
     loads = []
     for t in range(SLOTS):
@@ -93,6 +104,11 @@
     barrier = pltpu.get_barrier_semaphore()
     for neighbour in (left, right):
         pl.semaphore_signal(barrier, inc=1, device_id={"tile": neighbour}, device_id_type=MESH)
+    pl.semaphore_signal(barrier, inc=1, device_id=on_chip(place, 1 - core), device_id_type=MESH)
+    for axis in "xyz":
+        for distance in (1, 2, 3):
+            pl.semaphore_signal(
+                barrier, inc=1, device_id=along(axis, distance), device_id_type=MESH)
 
     zero8 = jnp.zeros((8, 128), F32)
 
@@ -107,15 +123,14 @@
     lax.fori_loop(0, SLOTS * SIDE, clear, 0)
 
     for a in range(3):
-        k0, k1, k2 = (ktop[a, b] for b in range(3))
-        wtop[a * 128 : a * 128 + 128, 0:128] = jnp.concatenate([k0, k2], axis=1)
-        wtop[a * 128 : a * 128 + 128, 128:256] = jnp.concatenate([k1, k1], axis=1)
-    zero_kernel = jnp.zeros((128, 64), F32)
-    for b in range(3):
-        first = jnp.concatenate([ktop[2, 2 - b], ktop[1, 2 - b]], axis=1).astype(F32)
-        last = jnp.concatenate([ktop[0, 2 - b].astype(F32), zero_kernel], axis=1)
-        wback[0:128, b * 128 : b * 128 + 128] = first.T.astype(BF16)
-        wback[128:256, b * 128 : b * 128 + 128] = last.T.astype(BF16)
+        outer = jnp.concatenate([ktop[a, 0], ktop[a, 2]], axis=0).astype(F32).T
+        centre = jnp.concatenate([ktop[a, 1], ktop[a, 1]], axis=0).astype(F32).T
+        wtop[a * 128 : a * 128 + 128, 0:128] = outer.astype(BF16)
+        wtop[a * 128 : a * 128 + 128, 128:256] = centre.astype(BF16)
+        for b in range(3):
+            wback[a * 64 : a * 64 + 64, b * 128 : b * 128 + 128] = ktop[2 - a, 2 - b]
+    wback[192:256, :] = jnp.zeros((64, 384), BF16)
+    btop_twice = jnp.concatenate([btop[...], btop[...]], axis=1)
 
     for copy in loads[:SLOTS]:
         copy.wait()
@@ -137,7 +152,7 @@
                 fsend[side, t * 2 + col, :, 0:128] = strip_a[at, :].astype(BF16)
                 fsend[side, t * 2 + col, :, 128:256] = strip_b[at, :].astype(BF16)
 
-    pl.semaphore_wait(barrier, 2)
+    pl.semaphore_wait(barrier, 12)
 
     def exchange(send, recv, at):
         copies = []
@@ -253,7 +268,7 @@
 
     def up_of(before, after, centre, cotangent):
         pair = jnp.where(low, before, after)
-        pre = pair + pltpu.roll(pair, 64, 1) + centre + btop[...]
+        pre = pair + pltpu.roll(pair, 64, 1) + centre + btop_twice
         gate = sigmoid(pre)
         value = pre * gate
         return value, cotangent * (gate + value * (1.0 - gate))
@@ -376,14 +391,15 @@
 
     bias_mid = lax.fori_loop(0, SLOTS * SIDE, slopes, jnp.zeros((8, 128), F32), unroll=4)
 
-    def shift_slope(r, _):
-        at = pl.ds(pl.multiple_of(r * SIDE, 16), SIDE)
-        ss[at, 0:128] = sf[pl.ds(r * FULL + 10, SIDE), :].astype(BF16)
-        ss[at, 128:256] = sf[pl.ds(pl.multiple_of(r * FULL + 8, 8), SIDE), :].astype(BF16)
-        ss[at, 256:384] = sf[pl.ds(r * FULL + 6, SIDE), :].astype(BF16)
-        return 0
-
-    lax.fori_loop(0, SLOTS * SIDE, shift_slope, 0, unroll=4)
+    def shift_slope(g, _):
+        at = pl.ds(pl.multiple_of(g * 128, 128), 128)
+        for b, first in enumerate((10, 8, 6)):
+            rows = [sf[pl.ds((g * 4 + k) * FULL + first, SIDE), :] for k in range(4)]
+            block = jnp.concatenate(rows, axis=0).astype(BF16)
+            sst[b * 128 : b * 128 + 128, at] = block.T
+        return 0
+
+    lax.fori_loop(0, SLOTS * SIDE // 4, shift_slope, 0)
     for t in range(SLOTS):
         for side, col, cell in columns:
             edge = scol_w if side == 0 else scol_e
@@ -391,28 +407,139 @@
             edge[at : at + 32, :] = sf[
                 pl.ds(t * SIDE * FULL + 8 + cell, SIDE, stride=FULL), :].astype(BF16)
 
-    acc_mid[0:128, :] = lax.dot_general(scol_w[...], sa_w[...], across, preferred_element_type=F32)
-    acc_mid[128:256, :] = jnp.zeros((128, 768), F32)
-    acc_mid[256:384, :] = lax.dot_general(scol_e[...], sa_e[...], across, preferred_element_type=F32)
-
-    def grad_mid(t, _):
-        rhs = jnp.concatenate([fp[t, 64 * a : 64 * a + CELLS, :] for a in range(3)], axis=1)
-        lhs = ss[pl.ds(pl.multiple_of(t * CELLS, 16), CELLS), :]
-        acc_mid[...] += lax.dot_general(lhs, rhs, across, preferred_element_type=F32)
-        return 0
-
-    lax.fori_loop(0, SLOTS, grad_mid, 0)
+    def send(chunk, at, src, dst, device):
+        copy = pltpu.make_async_remote_copy(
+            src_ref=src, dst_ref=dst, send_sem=sum_send.at[chunk, at],
+            recv_sem=sum_recv.at[chunk, at], device_id=device, device_id_type=MESH)
+        copy.start()
+        return copy
+
+    def reducer(chunk, order):
+        axes = tuple(order)
+        at = [place[axis] for axis in axes]
+        other = on_chip(place, 1 - core)
+        pending, started = [], []
+
+        def spread(base, axis_at, src_of, dst_of):
+            pending.clear()
+            for d in (1, 2, 3):
+                to = lax.rem(at[axis_at] + d, 4)
+                copy = send(chunk, base + d - 1, src_of(to), dst_of(d), along(axes[axis_at], d))
+                pending.append(copy)
+            started.extend(pending)
+
+        def arrive():
+            for copy in pending:
+                copy.wait_recv()
+
+        def rows_at(index, size):
+            return pl.ds(pl.multiple_of(index * size, 8), size)
+
+        def split_core():
+            sum_core[chunk] = grad[chunk].astype(BF16)
+            pending.clear()
+            pending.append(send(
+                chunk, 0, sum_core.at[chunk, rows_at(1 - core, 384)], core_in.at[chunk], other))
+            started.extend(pending)
+
+        def split_first():
+            arrive()
+            mine = grad[chunk, rows_at(core, 384), :]
+            first_out[chunk] = (mine + core_in[chunk].astype(F32)).astype(BF16)
+            spread(1, 0, lambda to: first_out.at[chunk, rows_at(to, 96)],
+                   lambda d: first_in.at[chunk, d - 1])
+
+        def split_second():
+            arrive()
+            value = first_out[chunk, rows_at(at[0], 96), :].astype(F32)
+            for d in range(3):
+                value = value + first_in[chunk, d].astype(F32)
+            second_out[chunk] = value
+            spread(4, 1, lambda to: second_out.at[chunk, rows_at(to, 24)],
+                   lambda d: second_in.at[chunk, d - 1])
+
+        def swap_third():
+            arrive()
+            value = second_out[chunk, rows_at(at[1], 24), :]
+            for d in range(3):
+                value = value + second_in[chunk, d]
+            third_in[chunk, at[2]] = value
+            spread(7, 2, lambda to: third_in.at[chunk, at[2]],
+                   lambda d: third_in.at[chunk, at[2]])
+
+        def back_second():
+            arrive()
+            value = third_in[chunk, 0] + third_in[chunk, 1]
+            value = value + (third_in[chunk, 2] + third_in[chunk, 3])
+            mine = rows_at(at[1], 24)
+            second_back[chunk, mine, :] = value
+            spread(10, 1, lambda to: second_back.at[chunk, mine],
+                   lambda d: second_back.at[chunk, mine])
+
+        def back_first():
+            arrive()
+            mine = rows_at(at[0], 96)
+            first_back[chunk, mine, :] = second_back[chunk].astype(BF16)
+            spread(13, 0, lambda to: first_back.at[chunk, mine],
+                   lambda d: first_back.at[chunk, mine])
+
+        def back_core():
+            arrive()
+            mine = rows_at(core, 384)
+            pending.clear()
+            pending.append(send(
+                chunk, 16, first_back.at[chunk], total.at[chunk, mine], other))
+            started.extend(pending)
+            total[chunk, mine, :] = first_back[chunk]
+
+        def finish():
+            arrive()
+            for copy in started:
+                copy.wait_send()
+
+        return iter((split_core, split_first, split_second, swap_third,
+                     back_second, back_first, back_core, finish))
+
+    reducers = [reducer(0, "zyx"), reducer(1, "xyz"), reducer(2, "yzx"), reducer(3, "zxy")]
+
+    def advance(*chunks):
+        for chunk in chunks:
+            step = next(reducers[chunk], None)
+            if step is not None:
+                step()
 
     for a in range(3):
         for b in range(3):
-            at = (a * 3 + b) * 256
-            grad[at : at + 256, :] = acc_mid[b * 128 : b * 128 + 128, a * 256 : a * 256 + 256].T
-        for half in range(2):
-            at = 2304 + half * 384 + a * 128
-            grad[at : at + 128, :] = acc_top[
-                half * 128 : half * 128 + 128, a * 128 : a * 128 + 128].T
-    grad[3072:3080, :] = bias_mid
-    grad[3080:3088, :] = bias_top
+            at = (a * 3 + b) * 64
+            grad[0, at : at + 64, :] = acc_top[b * 64 : b * 64 + 64, a * 128 : a * 128 + 128]
+    grad[0, 576:584, :] = bias_mid
+    grad[0, 584:592, :] = bias_top
+    grad[0, 592:768, :] = jnp.zeros((176, 128), F32)
+    advance(0)
+
+    for a in range(3):
+        parts = []
+        for t in range(SLOTS):
+            parts.append(jnp.dot(
+                sst[:, t * CELLS : t * CELLS + CELLS], fp[t, 64 * a : 64 * a + CELLS, :],
+                preferred_element_type=F32))
+        acc = (parts[0] + parts[1]) + (parts[2] + parts[3])
+        q = slice(a * 256, a * 256 + 256)
+        west = lax.dot_general(scol_w[...], sa_w[:, q], across, preferred_element_type=F32)
+        east = lax.dot_general(scol_e[...], sa_e[:, q], across, preferred_element_type=F32)
+        grad[1 + a, 0:256, :] = (acc[0:128] + west).T
+        grad[1 + a, 256:512, :] = acc[128:256].T
+        grad[1 + a, 512:768, :] = (acc[256:384] + east).T
+        advance(*range(a + 1, -1, -1))
+    for _ in range(7):
+        advance(0, 1, 2, 3)
+
+    for a in range(3):
+        gmid_out[a * 768 : a * 768 + 768, :] = total[1 + a]
+    gtop_out[...] = total[0, 0:576, :]
+    sums = total[0, 576:592, :].astype(F32)
+    bmid_out[...] = jnp.sum(sums[0:8], axis=0, keepdims=True)
+    btop_out[...] = jnp.sum(sums[8:16], axis=0, keepdims=True)[:, 0:64]
 
 
 def shards(features, cotangent, neighbors, live_count, kernel_mid, bias_mid, kernel_top, bias_top):
@@ -421,14 +548,17 @@
     smem = pl.BlockSpec(memory_space=pltpu.SMEM)
     hbm = pl.BlockSpec(memory_space=pl.ANY)
     rows = SLOTS * SIDE
-    out, grad = pl.pallas_call(
+    out, grad_mid, grad_top, bias_mid_sum, bias_top_sum = pl.pallas_call(
         kernel,
         out_shape=(
             jax.ShapeDtypeStruct((SLOTS, SIDE, 2048), BF16),
-            jax.ShapeDtypeStruct((3088, 128), F32),
+            jax.ShapeDtypeStruct((2304, 128), BF16),
+            jax.ShapeDtypeStruct((576, 128), BF16),
+            jax.ShapeDtypeStruct((1, 128), F32),
+            jax.ShapeDtypeStruct((1, 64), F32),
         ),
         in_specs=[hbm, hbm, smem, smem, hbm, vmem, vmem, vmem],
-        out_specs=(vmem, vmem),
+        out_specs=(vmem,) * 5,
         scratch_shapes=[
             pltpu.VMEM((SLOTS, PADDED, 256), BF16),
             pltpu.VMEM((SLOTS, PADDED, 128), BF16),
@@ -467,30 +597,37 @@
             pltpu.VMEM((256, 128), BF16),
             pltpu.VMEM((256, 128), BF16),
             pltpu.VMEM((rows * FULL, 128), F32),
-            pltpu.VMEM((rows * SIDE, 384), BF16),
-            pltpu.VMEM((384, 768), F32),
+            pltpu.VMEM((384, rows * SIDE), BF16),
             pltpu.VMEM((256, 384), F32),
             pltpu.VMEM((SLOTS, SIDE, 2048), BF16),
+            pltpu.VMEM((4, 768, 128), F32),
+            pltpu.VMEM((4, 768, 128), BF16),
+            pltpu.VMEM((4, 384, 128), BF16),
+            pltpu.VMEM((4, 384, 128), BF16),
+            pltpu.VMEM((4, 3, 96, 128), BF16),
+            pltpu.VMEM((4, 96, 128), F32),
+            pltpu.VMEM((4, 3, 24, 128), F32),
+            pltpu.VMEM((4, 4, 24, 128), F32),
+            pltpu.VMEM((4, 96, 128), F32),
+            pltpu.VMEM((4, 384, 128), BF16),
+            pltpu.VMEM((4, 768, 128), BF16),
             pltpu.SemaphoreType.DMA((14,)),
             pltpu.SemaphoreType.DMA((6,)),
             pltpu.SemaphoreType.DMA((6,)),
+            pltpu.SemaphoreType.DMA((4, 17)),
+            pltpu.SemaphoreType.DMA((4, 17)),
         ],
         compiler_params=pltpu.CompilerParams(
             collective_id=0, has_side_effects=True, vmem_limit_bytes=60 * 2**20),
         name="backend_layers",
     )(
         features.reshape(slots, side * side, channels), cotangent, neighbors, live_count,
-        kernel_mid, bias_mid.reshape(1, 128), kernel_top,
-        jnp.concatenate([bias_top, bias_top]).reshape(1, 128),
+        kernel_mid, bias_mid.reshape(1, 128), jnp.swapaxes(kernel_top, 2, 3),
+        bias_top.reshape(1, 64),
     )
-    grad = lax.psum(grad, ("rep", "tile"))
-    grad_mid = grad[:2304].reshape(3, 3, 256, 128)
-    low = grad[2304:2688].reshape(3, 128, 2, 64).transpose(0, 2, 1, 3)
-    high = grad[2688:3072, 0:64].reshape(3, 1, 128, 64)
-    grad_top = jnp.concatenate([low, high], axis=1)
-    bias_mid_sum = jnp.sum(grad[3072:3080], axis=0)
-    bias_top_sum = jnp.sum(grad[3080:3088, 0:64], axis=0)
-    return out, grad_mid, bias_mid_sum, grad_top, bias_top_sum
+    grad_mid = grad_mid.reshape(3, 3, 256, 128).astype(F32)
+    grad_top = jnp.swapaxes(grad_top.reshape(3, 3, 64, 128), 2, 3).astype(F32)
+    return out, grad_mid, bias_mid_sum.reshape(128), grad_top, bias_top_sum.reshape(64)
 
 
 def solution(mesh):

time: 209 us -> 77.2 us (0.37)
  waiting for transfers between devices: 152 us -> 0 us
  Pallas kernels: 33.2 us -> 70 us
  between operations: 14.7 us -> 1.31 us
  local copies, waits for them, and re-layouts: 6.73 us -> 1.83 us
    psum x1 -> x0, waiting for transfers between devices: 152 us -> none  [shards(): grad = lax.psum(grad, ('rep', 'tile'))]
    pallas_call x1, Pallas kernels: 33.2 us -> 70 us  [shards(): pl.pallas_call(kernel, out_shape=(jax.ShapeDtypeStruct((SLOTS, SIDE, 2048...]
    convert_element_type x0 -> x2, other arithmetic: none -> 3.87 us  [the longest x1 2.22 us: shards(): grad_mid = grad_mid.reshape(3, 3, 256, 128).astype(F32)]
    slice x4 -> x0, local copies, waits for them, and re-layouts: 3.19 us -> none  [the longest x2 1.16 us: shards(): low = grad[2304:2688].reshape(3, 128, 2, 64).transpose(0, 2, 1, 3)]
  transfers between devices with their start and end apart: 1 -> 0, of which waited for: 1 -> 0; matrix products, arithmetic and copies ran while one was open for 0% -> 0% of each run, Pallas kernels for 0% -> 0%
where the time goes in v1:
time: 77.2 us; the launch traced here: 77 us
  Pallas kernels  70 us (91%)
  other arithmetic  3.87 us (5%)
  local copies, waits for them, and re-layouts  1.83 us (2%)
  between operations  1.31 us (2%)
    pallas_call x1, Pallas kernels, shards(): pl.pallas_call(kernel, out_shape=(jax.ShapeDtypeStruct((SLOTS, SIDE, 2048...  70 us
    convert_element_type x1, other arithmetic, shards(): grad_mid = grad_mid.reshape(3, 3, 256, 128).astype(F32)  2.22 us
    unnamed x9, local copies, waits for them, and re-layouts  1.83 us
    convert_element_type x1, other arithmetic, shards(): grad_top = jnp.swapaxes(grad_top.reshape(3, 3, 64, 128), 2, 3).astype(F32)  1.65 us

profile of v1, /device:TPU:1, one launch (start us, length us, event | category | flops | bytes accessed | tf_op | source)
XLA Modules:
  0.0 77.0 jit_solution(15755655792781091278)
XLA Ops:
  1.3 70.0 %backend_layers.1 = (bf16[4,32,2048]{2,1,0:T(8,128)(2,1)}, bf16[2304,128]{1,0:T(8,128)(2,1)}, bf16[576,128]{1,0:T(8,128)(2,1)}, f32[1,128]{1,0:T(1,128)}, f32[1,64]{1,0:T(1,128)}) custom-call(bf16[4,1024,256]{2,1,0:T(8,128)(2,1)} %bitcast.12, bf16[4,32,2048]{2,1,0:T(8,128)(2,1)} %cot.1, s32[4,8]{1,0:T(4,128)} %nbr.1, s32[1]{0:T(128)S(6)} %copy.16.live, ...), custom_call_target="tpu_custom_call" | custom-call | tf_op jit(solution)/shard_map/backend_layers/pallas_call | solution.py:551
  71.3 0.0 copy-start
  71.3 0.0 copy-start.2
  71.3 0.0 copy-start.1
  71.3 2.2 %convert.3 = f32[3,3,256,128]{3,2,1,0:T(8,128)} convert(bf16[3,3,256,128]{3,2,1,0:T(8,128)(2,1)} %bitcast.13) | non-fusion elementwise | flops 294912 | bytes 1769472 | tf_op jit(solution)/shard_map/convert_element_type | solution.py:628
  73.5 1.6 %convert_bitcast_fusion = f32[3,3,128,64]{2,3,1,0:T(8,128)} fusion(bf16[3,3,64,128]{3,2,1,0:T(8,128)(2,1)} %bitcast.15), kind=kLoop, calls=%fused_computation | loop fusion | flops 73728 | bytes 442368 | tf_op jit(solution)/shard_map/convert_element_type | solution.py:629
  75.2 0.0 copy-done
  75.2 0.8 %copy.17 = bf16[4,32,2048]{2,1,0:T(8,128)(2,1)} copy(bf16[4,32,2048]{2,1,0:T(8,128)(2,1)S(1)} %copy-done) | data formatting | bytes 1048576
  76.0 0.0 copy-done.2
  76.0 0.5 copy.18
  76.5 0.0 copy-done.1
  76.5 0.5 copy.19
Async XLA Ops:
  71.3 3.9 %copy-start = (bf16[4,32,2048]{2,1,0:T(8,128)(2,1)S(1)}, bf16[4,32,2048]{2,1,0:T(8,128)(2,1)}, u32[]{:S(2)}) copy-start(bf16[4,32,2048]{2,1,0:T(8,128)(2,1)} %get-tuple-element.20) | copy-start | bytes 1572868
  71.3 4.7 %copy-start.2 = (f32[1,128]{1,0:T(1,128)S(1)}, f32[1,128]{1,0:T(1,128)}, u32[]{:S(2)}) copy-start(f32[1,128]{1,0:T(1,128)} %get-tuple-element.12) | copy-start | bytes 1540
  71.3 5.2 %copy-start.1 = (f32[1,64]{1,0:T(1,128)S(1)}, f32[1,64]{1,0:T(1,128)}, u32[]{:S(2)}) copy-start(f32[1,64]{1,0:T(1,128)} %get-tuple-element.14) | copy-start | bytes 772

commit v2 on v0

--- a/solution.py
+++ b/solution.py
@@ -65,16 +65,30 @@
 
 def kernel(
     feat, cot, nbr, live, kmid, bmid, ktop, btop,
-    out, grad,
+    out, sums,
     fp, hp, wmid, wtop, wback, y0, y1, y2, ya, yb, work, sa_w, sa_e, sh_w, sh_e, su_w, su_e,
     strip_a, strip_b, fsend, frecv, hsend, hrecv, usend, urecv,
-    slope, cots, outs, uf, uplo, uphi, uu, ucol_w, ucol_e, scol_w, scol_e, sf, ss,
-    acc_mid, acc_top, cotv,
-    local_sem, send_sem, recv_sem,
+    slope, uf, uplo, uphi, uut, ucol_w, ucol_e, scol_w, scol_e, sf,
+    sst, acc_mid, acc_top, cotv, grad, sum_core, core_in, plane_out, plane_in, line_in, total,
+    local_sem, send_sem, recv_sem, sum_send, sum_recv,
 ):
     n = lax.axis_size("tile")
     me = lax.axis_index("tile")
     right, left = lax.rem(me + 1, n), lax.rem(me + n - 1, n)
+    z, y, x, core = lax.axis_index("rep"), me // 8, lax.rem(me // 2, 4), lax.rem(me, 2)
+    place = {"x": x, "y": y, "z": z}
+
+    def on_chip(where, c):
+        return {"rep": where["z"], "tile": where["y"] * 8 + where["x"] * 2 + c}
+
+    def moved(steps):
+        there = dict(place)
+        for axis, distance in steps:
+            there[axis] = lax.rem(place[axis] + distance, 4)
+        return there
+
+    corners = [(d, e) for d in range(4) for e in range(4) if d or e]
+    orders = ("xyz", "yzx", "zxy")
 
     loads = []
     for t in range(SLOTS):
@@ -93,29 +107,13 @@
     barrier = pltpu.get_barrier_semaphore()
     for neighbour in (left, right):
         pl.semaphore_signal(barrier, inc=1, device_id={"tile": neighbour}, device_id_type=MESH)
-
-    zero8 = jnp.zeros((8, 128), F32)
-
-    def clear(r, _):
-        base = pl.multiple_of(r * FULL, 8)
-        uf[pl.ds(base, 8), :] = zero8
-        uf[pl.ds(base + 40, 8), :] = zero8
-        sf[pl.ds(base, 8), :] = zero8
-        sf[pl.ds(base + 40, 8), :] = zero8
-        return 0
-
-    lax.fori_loop(0, SLOTS * SIDE, clear, 0)
-
-    for a in range(3):
-        k0, k1, k2 = (ktop[a, b] for b in range(3))
-        wtop[a * 128 : a * 128 + 128, 0:128] = jnp.concatenate([k0, k2], axis=1)
-        wtop[a * 128 : a * 128 + 128, 128:256] = jnp.concatenate([k1, k1], axis=1)
-    zero_kernel = jnp.zeros((128, 64), F32)
-    for b in range(3):
-        first = jnp.concatenate([ktop[2, 2 - b], ktop[1, 2 - b]], axis=1).astype(F32)
-        last = jnp.concatenate([ktop[0, 2 - b].astype(F32), zero_kernel], axis=1)
-        wback[0:128, b * 128 : b * 128 + 128] = first.T.astype(BF16)
-        wback[128:256, b * 128 : b * 128 + 128] = last.T.astype(BF16)
+    pl.semaphore_signal(barrier, inc=1, device_id=on_chip(place, 1 - core), device_id_type=MESH)
+    for first, second, _ in orders:
+        for d, e in corners:
+            if d:
+                pl.semaphore_signal(
+                    barrier, inc=1, device_id=on_chip(moved(((first, d), (second, e))), core),
+                    device_id_type=MESH)
 
     for copy in loads[:SLOTS]:
         copy.wait()
@@ -130,14 +128,14 @@
             strip_b[pl.ds(at, 8), :] = rows[:, 128:256]
             return 0
 
-        lax.fori_loop(0, SLOTS * SIDE, gather, 0, unroll=4)
+        lax.fori_loop(0, SLOTS * SIDE, gather, 0, unroll=16)
         for t in range(SLOTS):
             for col, pick in enumerate(picks):
                 at = pl.ds(t * 256 + pick, 32, stride=8)
                 fsend[side, t * 2 + col, :, 0:128] = strip_a[at, :].astype(BF16)
                 fsend[side, t * 2 + col, :, 128:256] = strip_b[at, :].astype(BF16)
 
-    pl.semaphore_wait(barrier, 2)
+    pl.semaphore_wait(barrier, 39)
 
     def exchange(send, recv, at):
         copies = []
@@ -152,6 +150,28 @@
 
     feature_copies = exchange(fsend, frecv, 0)
 
+    zero8 = jnp.zeros((8, 128), F32)
+
+    def clear(r, _):
+        base = pl.multiple_of(r * FULL, 8)
+        uf[pl.ds(base, 8), :] = zero8
+        uf[pl.ds(base + 40, 8), :] = zero8
+        sf[pl.ds(base, 8), :] = zero8
+        sf[pl.ds(base + 40, 8), :] = zero8
+        return 0
+
+    lax.fori_loop(0, SLOTS * SIDE, clear, 0, unroll=8)
+
+    for a in range(3):
+        outer = jnp.concatenate([ktop[a, 0], ktop[a, 2]], axis=0).astype(F32).T
+        centre = jnp.concatenate([ktop[a, 1], ktop[a, 1]], axis=0).astype(F32).T
+        wtop[a * 128 : a * 128 + 128, 0:128] = outer.astype(BF16)
+        wtop[a * 128 : a * 128 + 128, 128:256] = centre.astype(BF16)
+        for b in range(3):
+            wback[a * 64 : a * 64 + 64, b * 128 : b * 128 + 128] = ktop[2 - a, 2 - b]
+    wback[192:256, :] = jnp.zeros((64, 384), BF16)
+    btop_twice = jnp.concatenate([btop[...], btop[...]], axis=1)
+
     fill_bands(fp, nbr)
     for copy in loads[SLOTS:]:
         copy.wait()
@@ -170,13 +190,6 @@
     lax.fori_loop(0, SLOTS, conv_mid, 0)
 
     low = low_lanes((SIDE, 128))
-    for t in range(SLOTS):
-        for pair in range(SIDE // 2):
-            x = cotv[t, :, pair * 128 : pair * 128 + 128].astype(F32)
-            turned = pltpu.roll(x, 64, 1)
-            cots[pl.ds(t * CELLS + 2 * pair, SIDE, stride=SIDE), :] = jnp.where(low, x, turned)
-            cots[pl.ds(t * CELLS + 2 * pair + 1, SIDE, stride=SIDE), :] = jnp.where(low, turned, x)
-
     for copy in feature_copies:
         copy.wait()
     margin_strips(frecv.at[0], nbr, 0, 3, 5, work, sa_w, 256)
@@ -251,68 +264,73 @@
             ya[pl.ds(t * SIDE * FULL + 6 + col, SIDE, stride=FULL), :] = west[rows]
             ya[pl.ds(t * SIDE * FULL + 40 + col, SIDE, stride=FULL), :] = east[rows]
 
-    def up_of(before, after, centre, cotangent):
-        pair = jnp.where(low, before, after)
-        pre = pair + pltpu.roll(pair, 64, 1) + centre + btop[...]
+    zero_rows = jnp.zeros((SIDE, 128), F32)
+
+    def up_pair(t, pair, mask):
+        cell = 2 * pair
+        base = t * SIDE * FULL
+        before = [ya[pl.ds(base + 6 + cell + k, SIDE, stride=FULL), :] for k in range(2)]
+        after = [ya[pl.ds(base + 10 + cell + k, SIDE, stride=FULL), :] for k in range(2)]
+        centre = [yb[pl.ds(t * CELLS + cell + k, SIDE, stride=SIDE), :] for k in range(2)]
+        pre = jnp.where(low, before[0], after[1])
+        pre = pre + pltpu.roll(jnp.where(low, before[1], after[0]), 64, 1)
+        pre = pre + jnp.where(low, centre[0], centre[1]) + btop_twice
         gate = sigmoid(pre)
         value = pre * gate
-        return value, cotangent * (gate + value * (1.0 - gate))
-
-    zero_rows = jnp.zeros((SIDE, 128), F32)
+        lanes = pl.ds(pair * 128, 128)
+        if not isinstance(pair, int):
+            lanes = pl.ds(pl.multiple_of(pair * 128, 128), 128)
+        out[t, :, lanes] = (value * mask).astype(BF16)
+        up = cotv[t, :, lanes].astype(F32) * (gate + value * (1.0 - gate)) * mask
+        up = up.astype(BF16).astype(F32)
+        turned = pltpu.roll(up, 64, 1)
+        uf[pl.ds(base + 8 + cell, SIDE, stride=FULL), :] = jnp.where(low, up, turned)
+        uf[pl.ds(base + 9 + cell, SIDE, stride=FULL), :] = jnp.where(low, turned, up)
+        return up, turned
+
+    def tile_sum(up):
+        return jnp.sum(up.reshape(4, 8, 128), axis=0)
+
+    bias_top = jnp.zeros((8, 128), F32)
     for t in range(SLOTS):
-        for side in range(2):
-            ups = []
-            for col in range(2):
-                cell = 30 * side + col
-                _, up = up_of(
-                    ya[pl.ds(t * SIDE * FULL + 6 + cell, SIDE, stride=FULL), :],
-                    ya[pl.ds(t * SIDE * FULL + 10 + cell, SIDE, stride=FULL), :],
-                    yb[pl.ds(t * CELLS + cell, SIDE, stride=SIDE), :],
-                    cots[pl.ds(t * CELLS + cell, SIDE, stride=SIDE), :])
-                up = up * alive[t]
-                ups.append(up)
-                edge = ucol_w if side == 0 else ucol_e
+        for side, edge in enumerate((ucol_w, ucol_e)):
+            up, turned = up_pair(t, 15 * side, alive[t])
+            usend[side, t] = up.astype(BF16)
+            for col, rows in enumerate((up, turned)):
                 at = (t * 2 + col) * 32
-                edge[at : at + 32, :] = jnp.where(low, up, zero_rows).astype(BF16)
-            usend[side, t] = jnp.where(low, ups[0], ups[1]).astype(BF16)
+                edge[at : at + 32, :] = jnp.where(low, rows, zero_rows).astype(BF16)
+            bias_top = bias_top + tile_sum(up)
     upstream_copies = exchange(usend, urecv, 4)
 
-    def top_rows(r, total):
-        t, i = r // SIDE, r % SIDE
+    def top_pairs(r, total):
+        t, pair = r // 14, lax.rem(r, 14) + 1
         mask = jnp.where(t < live[0], 1.0, 0.0).astype(F32)
-        value, up = up_of(
-            ya[pl.ds(r * FULL + 6, SIDE), :],
-            ya[pl.ds(r * FULL + 10, SIDE), :],
-            yb[pl.ds(pl.multiple_of(r * SIDE, 8), SIDE), :],
-            cots[pl.ds(pl.multiple_of(r * SIDE, 8), SIDE), :])
-        outs[pl.ds(pl.multiple_of(r * SIDE, 8), SIDE), :] = value * mask
-        up = (up * mask).astype(BF16).astype(F32)
-        uf[pl.ds(pl.multiple_of(r * FULL + 8, 8), SIDE), :] = up
-        at = pl.ds(pl.multiple_of(64 + i * SIDE, 16), SIDE)
-        uplo[t, at, :] = jnp.where(low, up, zero_rows).astype(BF16)
-        uphi[t, at, :] = jnp.where(low, zero_rows, up).astype(BF16)
-        return total + jnp.sum(up.reshape(4, 8, 128), axis=0)
-
-    bias_top = lax.fori_loop(0, SLOTS * SIDE, top_rows, jnp.zeros((8, 128), F32), unroll=4)
+        up, _ = up_pair(t, pair, mask)
+        return total + tile_sum(up)
+
+    bias_top = lax.fori_loop(0, SLOTS * 14, top_pairs, bias_top, unroll=7)
+
+    def shift_up(g, _):
+        at = pl.ds(pl.multiple_of(g * 128, 128), 128)
+        t, quarter = g // 8, lax.rem(g, 8)
+
+        def cells(first):
+            return jnp.concatenate(
+                [uf[pl.ds((g * 4 + k) * FULL + first, SIDE), :] for k in range(4)], axis=0)
+
+        left_half = low_lanes((128, 128))
+        zero = jnp.zeros((128, 128), F32)
+        same = cells(8)
+        rows = pl.ds(pl.multiple_of(64 + quarter * 128, 16), 128)
+        uplo[t, rows, :] = jnp.where(left_half, same, zero).astype(BF16)
+        uphi[t, rows, :] = jnp.where(left_half, zero, same).astype(BF16)
+        uut[0:128, at] = jnp.where(left_half, cells(10), same).astype(BF16).T
+        uut[128:192, at] = cells(6).astype(BF16).T[0:64]
+        return 0
+
+    lax.fori_loop(0, SLOTS * SIDE // 4, shift_up, 0, unroll=4)
     fill_bands(uplo, nbr)
     fill_bands(uphi, nbr)
-
-    def shift_up(r, _):
-        before = uf[pl.ds(r * FULL + 6, SIDE), :]
-        same = uf[pl.ds(pl.multiple_of(r * FULL + 8, 8), SIDE), :]
-        after = uf[pl.ds(r * FULL + 10, SIDE), :]
-        at = pl.ds(pl.multiple_of(r * SIDE, 16), SIDE)
-        uu[at, 0:128] = jnp.where(low, after, same).astype(BF16)
-        uu[at, 128:256] = before.astype(BF16)
-        return 0
-
-    lax.fori_loop(0, SLOTS * SIDE, shift_up, 0, unroll=4)
-
-    for t in range(SLOTS):
-        for pair in range(SIDE // 2):
-            x0 = outs[pl.ds(t * CELLS + 2 * pair, SIDE, stride=SIDE), :]
-            x1 = outs[pl.ds(t * CELLS + 2 * pair + 1, SIDE, stride=SIDE), :]
-            out[t, :, pair * 128 : pair * 128 + 128] = jnp.where(low, x0, x1).astype(BF16)
 
     zero_cols = jnp.zeros((256, 128), BF16)
     edges_l = jnp.concatenate([
@@ -320,12 +338,13 @@
         jnp.concatenate([zero_cols, ucol_e[...]], axis=1)], axis=0)
     edges_r = jnp.concatenate([sh_w[...], sh_e[...]], axis=0)
     across = (((0,), (0,)), ((), ()))
-    acc_top[...] = lax.dot_general(edges_l, edges_r, across, preferred_element_type=F32)
+    edges = lax.dot_general(edges_l, edges_r, across, preferred_element_type=F32)
+    acc_top[...] = edges[0:192]
 
     def grad_top(t, _):
         rhs = jnp.concatenate([hp[t, 64 * a : 64 * a + CELLS, :] for a in range(3)], axis=1)
-        lhs = uu[pl.ds(pl.multiple_of(t * CELLS, 16), CELLS), :]
-        acc_top[...] += lax.dot_general(lhs, rhs, across, preferred_element_type=F32)
+        lhs = uut[:, pl.ds(pl.multiple_of(t * CELLS, 128), CELLS)]
+        acc_top[...] += jnp.dot(lhs, rhs, preferred_element_type=F32)
         return 0
 
     lax.fori_loop(0, SLOTS, grad_top, 0)
@@ -376,14 +395,15 @@
 
     bias_mid = lax.fori_loop(0, SLOTS * SIDE, slopes, jnp.zeros((8, 128), F32), unroll=4)
 
-    def shift_slope(r, _):
-        at = pl.ds(pl.multiple_of(r * SIDE, 16), SIDE)
-        ss[at, 0:128] = sf[pl.ds(r * FULL + 10, SIDE), :].astype(BF16)
-        ss[at, 128:256] = sf[pl.ds(pl.multiple_of(r * FULL + 8, 8), SIDE), :].astype(BF16)
-        ss[at, 256:384] = sf[pl.ds(r * FULL + 6, SIDE), :].astype(BF16)
-        return 0
-
-    lax.fori_loop(0, SLOTS * SIDE, shift_slope, 0, unroll=4)
+    def shift_slope(g, _):
+        at = pl.ds(pl.multiple_of(g * 128, 128), 128)
+        for b, first in enumerate((10, 8, 6)):
+            rows = [sf[pl.ds((g * 4 + k) * FULL + first, SIDE), :] for k in range(4)]
+            block = jnp.concatenate(rows, axis=0).astype(BF16)
+            sst[b * 128 : b * 128 + 128, at] = block.T
+        return 0
+
+    lax.fori_loop(0, SLOTS * SIDE // 4, shift_slope, 0, unroll=4)
     for t in range(SLOTS):
         for side, col, cell in columns:
             edge = scol_w if side == 0 else scol_e
@@ -391,28 +411,139 @@
             edge[at : at + 32, :] = sf[
                 pl.ds(t * SIDE * FULL + 8 + cell, SIDE, stride=FULL), :].astype(BF16)
 
-    acc_mid[0:128, :] = lax.dot_general(scol_w[...], sa_w[...], across, preferred_element_type=F32)
-    acc_mid[128:256, :] = jnp.zeros((128, 768), F32)
-    acc_mid[256:384, :] = lax.dot_general(scol_e[...], sa_e[...], across, preferred_element_type=F32)
-
-    def grad_mid(t, _):
-        rhs = jnp.concatenate([fp[t, 64 * a : 64 * a + CELLS, :] for a in range(3)], axis=1)
-        lhs = ss[pl.ds(pl.multiple_of(t * CELLS, 16), CELLS), :]
-        acc_mid[...] += lax.dot_general(lhs, rhs, across, preferred_element_type=F32)
-        return 0
-
-    lax.fori_loop(0, SLOTS, grad_mid, 0)
+    def reducer(chunk, order):
+        base = chunk * 1024
+        first, second, third = order
+        shard = place[first] * 4 + place[second]
+        other = on_chip(place, 1 - core)
+        pending, started = [], []
+
+        def send(at, src, dst, device):
+            copy = pltpu.make_async_remote_copy(
+                src_ref=src, dst_ref=dst, send_sem=sum_send.at[chunk, at],
+                recv_sem=sum_recv.at[chunk, at], device_id=device, device_id_type=MESH)
+            copy.start()
+            pending.append(copy)
+            started.append(copy)
+
+        def arrive():
+            for copy in pending:
+                copy.wait_recv()
+            pending.clear()
+
+        def rows_at(index, size, offset=0):
+            return pl.ds(pl.multiple_of(offset + index * size, 16), size)
+
+        def split_core():
+            sum_core[chunk] = grad[base : base + 1024, :].astype(BF16)
+            send(0, sum_core.at[chunk, rows_at(1 - core, 512)], core_in.at[chunk], other)
+
+        def split_plane():
+            arrive()
+            mine = grad[rows_at(core, 512, base), :]
+            plane_out[chunk] = (mine + core_in[chunk].astype(F32)).astype(BF16)
+            for k, (d, e) in enumerate(corners):
+                there = moved(((first, d), (second, e)))
+                to = there[first] * 4 + there[second]
+                send(1 + k, plane_out.at[chunk, rows_at(to, 32)], plane_in.at[chunk, k],
+                     on_chip(there, core))
+
+        def swap_line():
+            arrive()
+            value = plane_out[chunk, rows_at(shard, 32), :].astype(F32)
+            for k in range(15):
+                value = value + plane_in[chunk, k].astype(F32)
+            mine = place[third]
+            line_in[chunk, mine] = value
+            for d in (1, 2, 3):
+                send(15 + d, line_in.at[chunk, mine], line_in.at[chunk, mine],
+                     on_chip(moved(((third, d),)), core))
+
+        def back_plane():
+            arrive()
+            value = line_in[chunk, 0] + line_in[chunk, 1]
+            value = value + (line_in[chunk, 2] + line_in[chunk, 3])
+            mine = rows_at(core * 16 + shard, 32, base)
+            total[mine, :] = value.astype(BF16)
+            for k, (d, e) in enumerate(corners):
+                send(19 + k, total.at[mine], total.at[mine],
+                     on_chip(moved(((first, d), (second, e))), core))
+
+        def back_core():
+            arrive()
+            half = rows_at(core, 512, base)
+            send(34, total.at[half], total.at[half], other)
+
+        def finish():
+            arrive()
+            for copy in started:
+                copy.wait_send()
+
+        return iter((split_core, split_plane, swap_line, back_plane, back_core, finish))
+
+    reducers = [reducer(chunk, order) for chunk, order in enumerate(orders)]
+
+    def advance(*chunks):
+        for chunk in chunks:
+            step = next(reducers[chunk], None)
+            if step is not None:
+                step()
 
     for a in range(3):
         for b in range(3):
-            at = (a * 3 + b) * 256
-            grad[at : at + 256, :] = acc_mid[b * 128 : b * 128 + 128, a * 256 : a * 256 + 256].T
-        for half in range(2):
-            at = 2304 + half * 384 + a * 128
-            grad[at : at + 128, :] = acc_top[
-                half * 128 : half * 128 + 128, a * 128 : a * 128 + 128].T
-    grad[3072:3080, :] = bias_mid
-    grad[3080:3088, :] = bias_top
+            at = (a * 3 + b) * 64
+            grad[at : at + 64, :] = acc_top[b * 64 : b * 64 + 64, a * 128 : a * 128 + 128]
+    grad[576:584, :] = bias_mid
+    grad[584:592, :] = bias_top
+    grad[592:768, :] = jnp.zeros((176, 128), F32)
+
+    for a in range(3):
+        q = slice(a * 256, a * 256 + 256)
+        acc_mid[0:128, :] = lax.dot_general(
+            scol_w[...], sa_w[:, q], across, preferred_element_type=F32)
+        acc_mid[128:256, :] = jnp.zeros((128, 256), F32)
+        acc_mid[256:384, :] = lax.dot_general(
+            scol_e[...], sa_e[:, q], across, preferred_element_type=F32)
+
+        def grad_mid(t, _):
+            acc_mid[...] += jnp.dot(
+                sst[:, pl.ds(pl.multiple_of(t * CELLS, 128), CELLS)],
+                fp[t, 64 * a : 64 * a + CELLS, :], preferred_element_type=F32)
+            return 0
+
+        lax.fori_loop(0, SLOTS, grad_mid, 0)
+        for b in range(3):
+            at = 768 + (a * 3 + b) * 256
+            grad[at : at + 256, :] = acc_mid[b * 128 : b * 128 + 128, :].T
+        advance(*((0,), (1, 0), (2, 1, 2))[a])
+    for _ in range(4):
+        advance(0, 1, 2)
+
+    sums[...] = total[...]
+
+
+def finish_kernel(sums, out_in, gmid, gtop, bmid, btop, out, mid_half, mid_full, top_half, out_held, sem):
+    whole = pltpu.make_async_copy(out_in, out_held, sem.at[0])
+    top = pltpu.make_async_copy(sums.at[pl.ds(0, 592)], top_half, sem.at[1])
+    mid = pltpu.make_async_copy(sums.at[pl.ds(768, 2304)], mid_half, sem.at[2])
+    mid.start()
+    whole.start()
+    top.start()
+    mid.wait()
+    mid_full[...] = mid_half[...].astype(F32)
+    mid_back = pltpu.make_async_copy(mid_full, gmid, sem.at[3])
+    mid_back.start()
+    whole.wait()
+    whole_back = pltpu.make_async_copy(out_held, out, sem.at[4])
+    whole_back.start()
+    top.wait()
+    gtop[...] = top_half[0:576, :].astype(F32)
+    tail = top_half[576:592, :].astype(F32)
+    bmid[...] = jnp.sum(tail[0:8], axis=0, keepdims=True)
+    twice = jnp.sum(tail[8:16], axis=0, keepdims=True)
+    btop[...] = twice[:, 0:64] + twice[:, 64:128]
+    mid_back.wait()
+    whole_back.wait()
 
 
 def shards(features, cotangent, neighbors, live_count, kernel_mid, bias_mid, kernel_top, bias_top):
@@ -421,11 +552,11 @@
     smem = pl.BlockSpec(memory_space=pltpu.SMEM)
     hbm = pl.BlockSpec(memory_space=pl.ANY)
     rows = SLOTS * SIDE
-    out, grad = pl.pallas_call(
+    out, sums = pl.pallas_call(
         kernel,
         out_shape=(
             jax.ShapeDtypeStruct((SLOTS, SIDE, 2048), BF16),
-            jax.ShapeDtypeStruct((3088, 128), F32),
+            jax.ShapeDtypeStruct((3072, 128), BF16),
         ),
         in_specs=[hbm, hbm, smem, smem, hbm, vmem, vmem, vmem],
         out_specs=(vmem, vmem),
@@ -456,41 +587,64 @@
             pltpu.VMEM((2, 4, 32, 128), BF16),
             pltpu.VMEM((2, 4, 32, 128), BF16),
             pltpu.VMEM((rows * SIDE, 128), F32),
-            pltpu.VMEM((rows * SIDE, 128), F32),
-            pltpu.VMEM((rows * SIDE, 128), F32),
             pltpu.VMEM((rows * FULL, 128), F32),
             pltpu.VMEM((SLOTS, PADDED, 128), BF16),
             pltpu.VMEM((SLOTS, PADDED, 128), BF16),
-            pltpu.VMEM((rows * SIDE, 256), BF16),
+            pltpu.VMEM((192, rows * SIDE), BF16),
             pltpu.VMEM((256, 128), BF16),
             pltpu.VMEM((256, 128), BF16),
             pltpu.VMEM((256, 128), BF16),
             pltpu.VMEM((256, 128), BF16),
             pltpu.VMEM((rows * FULL, 128), F32),
-            pltpu.VMEM((rows * SIDE, 384), BF16),
-            pltpu.VMEM((384, 768), F32),
-            pltpu.VMEM((256, 384), F32),
+            pltpu.VMEM((384, rows * SIDE), BF16),
+            pltpu.VMEM((384, 256), F32),
+            pltpu.VMEM((192, 384), F32),
             pltpu.VMEM((SLOTS, SIDE, 2048), BF16),
+            pltpu.VMEM((3072, 128), F32),
+            pltpu.VMEM((3, 1024, 128), BF16),
+            pltpu.VMEM((3, 512, 128), BF16),
+            pltpu.VMEM((3, 512, 128), BF16),
+            pltpu.VMEM((3, 15, 32, 128), BF16),
+            pltpu.VMEM((3, 4, 32, 128), F32),
+            pltpu.VMEM((3072, 128), BF16),
             pltpu.SemaphoreType.DMA((14,)),
             pltpu.SemaphoreType.DMA((6,)),
             pltpu.SemaphoreType.DMA((6,)),
+            pltpu.SemaphoreType.DMA((3, 35)),
+            pltpu.SemaphoreType.DMA((3, 35)),
         ],
         compiler_params=pltpu.CompilerParams(
             collective_id=0, has_side_effects=True, vmem_limit_bytes=60 * 2**20),
         name="backend_layers",
     )(
         features.reshape(slots, side * side, channels), cotangent, neighbors, live_count,
-        kernel_mid, bias_mid.reshape(1, 128), kernel_top,
-        jnp.concatenate([bias_top, bias_top]).reshape(1, 128),
+        kernel_mid, bias_mid.reshape(1, 128), jnp.swapaxes(kernel_top, 2, 3),
+        bias_top.reshape(1, 64),
     )
-    grad = lax.psum(grad, ("rep", "tile"))
-    grad_mid = grad[:2304].reshape(3, 3, 256, 128)
-    low = grad[2304:2688].reshape(3, 128, 2, 64).transpose(0, 2, 1, 3)
-    high = grad[2688:3072, 0:64].reshape(3, 1, 128, 64)
-    grad_top = jnp.concatenate([low, high], axis=1)
-    bias_mid_sum = jnp.sum(grad[3072:3080], axis=0)
-    bias_top_sum = jnp.sum(grad[3080:3088, 0:64], axis=0)
-    return out, grad_mid, bias_mid_sum, grad_top, bias_top_sum
+    grad_mid, grad_top, bias_mid_sum, bias_top_sum, out = pl.pallas_call(
+        finish_kernel,
+        out_shape=(
+            jax.ShapeDtypeStruct((2304, 128), F32),
+            jax.ShapeDtypeStruct((576, 128), F32),
+            jax.ShapeDtypeStruct((1, 128), F32),
+            jax.ShapeDtypeStruct((1, 64), F32),
+            jax.ShapeDtypeStruct((SLOTS, SIDE, 2048), BF16),
+        ),
+        in_specs=[hbm, hbm],
+        out_specs=(hbm, vmem, vmem, vmem, hbm),
+        scratch_shapes=[
+            pltpu.VMEM((2304, 128), BF16),
+            pltpu.VMEM((2304, 128), F32),
+            pltpu.VMEM((592, 128), BF16),
+            pltpu.VMEM((SLOTS, SIDE, 2048), BF16),
+            pltpu.SemaphoreType.DMA((5,)),
+        ],
+        compiler_params=pltpu.CompilerParams(vmem_limit_bytes=60 * 2**20),
+        name="finish",
+    )(sums, out)
+    grad_mid = grad_mid.reshape(3, 3, 256, 128)
+    grad_top = jnp.swapaxes(grad_top.reshape(3, 3, 64, 128), 2, 3)
+    return out, grad_mid, bias_mid_sum.reshape(128), grad_top, bias_top_sum.reshape(64)
 
 
 def solution(mesh):

time: 209 us -> 60.1 us (0.29)
  waiting for transfers between devices: 152 us -> 0 us
  Pallas kernels: 33.2 us -> 58.6 us
  between operations: 14.7 us -> 1.29 us
  local copies, waits for them, and re-layouts: 6.73 us -> 0 us
  other arithmetic: 2.46 us -> 0 us
    psum x1 -> x0, waiting for transfers between devices: 152 us -> none  [shards(): grad = lax.psum(grad, ('rep', 'tile'))]
    pallas_call x1, Pallas kernels: 33.2 us -> 55.5 us  [shards(): pl.pallas_call(kernel, out_shape=(jax.ShapeDtypeStruct((SLOTS, SIDE, 2048...]
    unnamed x7 -> x0, local copies, waits for them, and re-layouts: 3.34 us -> none
    slice x4 -> x0, local copies, waits for them, and re-layouts: 3.19 us -> none  [the longest x2 1.16 us: shards(): low = grad[2304:2688].reshape(3, 128, 2, 64).transpose(0, 2, 1, 3)]
    pallas_call x0 -> x1, Pallas kernels: none -> 3.09 us  [shards(): pl.pallas_call(finish_kernel, out_shape=(jax.ShapeDtypeStruct((2304, 128)...]
  transfers between devices with their start and end apart: 1 -> 0, of which waited for: 1 -> 0; matrix products, arithmetic and copies ran while one was open for 0% -> 0% of each run, Pallas kernels for 0% -> 0%
where the time goes in v2:
time: 60.1 us; the launch traced here: 59.9 us
  Pallas kernels  58.6 us (98%)
  between operations  1.29 us (2%)
    pallas_call x1, Pallas kernels, shards(): pl.pallas_call(kernel, out_shape=(jax.ShapeDtypeStruct((SLOTS, SIDE, 2048...  55.5 us
    pallas_call x1, Pallas kernels, shards(): pl.pallas_call(finish_kernel, out_shape=(jax.ShapeDtypeStruct((2304, 128)...  3.09 us

profile of v2, /device:TPU:1, one launch (start us, length us, event | category | flops | bytes accessed | tf_op | source)
XLA Modules:
  0.0 59.9 jit_solution(8243046107366321136)
XLA Ops:
  1.3 55.5 %backend_layers.1 = (bf16[4,32,2048]{2,1,0:T(8,128)(2,1)}, bf16[3072,128]{1,0:T(8,128)(2,1)}) custom-call(bf16[4,1024,256]{2,1,0:T(8,128)(2,1)} %bitcast.10, bf16[4,32,2048]{2,1,0:T(8,128)(2,1)} %cot.1, s32[4,8]{1,0:T(4,128)} %nbr.1, s32[1]{0:T(128)S(6)} %copy.13.live, bf16[3,3,256,128]{3,2,1,0:T(8,128)(2,1)} %kmid.1, f32[1,128]{1,0:T(1,128)} %bitcast.12, ...), custom_call_target="tpu_custom_call" | custom-call | tf_op jit(solution)/shard_map/backend_layers/pallas_call | solution.py:555
  56.8 3.1 %finish.1 = (f32[2304,128]{1,0:T(8,128)}, f32[576,128]{1,0:T(8,128)}, f32[1,128]{1,0:T(1,128)}, f32[1,64]{1,0:T(1,128)}, bf16[4,32,2048]{2,1,0:T(8,128)(2,1)}) custom-call(bf16[3072,128]{1,0:T(8,128)(2,1)} %get-tuple-element.12.sums, bf16[4,32,2048]{2,1,0:T(8,128)(2,1)} %get-tuple-element.13.out_in), custom_call_target="tpu_custom_call" | custom-call | tf_op jit(solution)/shard_map/finish/pallas_call | solution.py:624

commit v3 on v2

--- a/solution.py
+++ b/solution.py
@@ -15,8 +15,10 @@
 SIDE = 32
 CELLS = SIDE * SIDE
 PADDED = CELLS + 128
-WIDE = 40
 FULL = 48
+ODD_FULL = 49
+ODD_WIDE = 41
+ODD_SIDE = 33
 
 
 def sigmoid(v):
@@ -69,7 +71,7 @@
     fp, hp, wmid, wtop, wback, y0, y1, y2, ya, yb, work, sa_w, sa_e, sh_w, sh_e, su_w, su_e,
     strip_a, strip_b, fsend, frecv, hsend, hrecv, usend, urecv,
     slope, uf, uplo, uphi, uut, ucol_w, ucol_e, scol_w, scol_e, sf,
-    sst, acc_mid, acc_top, cotv, grad, sum_core, core_in, plane_out, plane_in, line_in, total,
+    sst, acc_top, cotv, outv, grad, core_in, plane_out, plane_in, line_in, total,
     local_sem, send_sem, recv_sem, sum_send, sum_recv,
 ):
     n = lax.axis_size("tile")
@@ -123,7 +125,7 @@
             t, i = r // SIDE, r % SIDE
             rows = fp[t, pl.ds(pl.multiple_of(64 + i * SIDE + cells, 16), 16), :].astype(F32)
             rows = rows[0:8] if cells == 0 else rows[8:16]
-            at = pl.multiple_of(r * 8, 8)
+            at = r * 9
             strip_a[pl.ds(at, 8), :] = rows[:, 0:128]
             strip_b[pl.ds(at, 8), :] = rows[:, 128:256]
             return 0
@@ -131,7 +133,7 @@
         lax.fori_loop(0, SLOTS * SIDE, gather, 0, unroll=16)
         for t in range(SLOTS):
             for col, pick in enumerate(picks):
-                at = pl.ds(t * 256 + pick, 32, stride=8)
+                at = pl.ds(t * 288 + pick, 32, stride=9)
                 fsend[side, t * 2 + col, :, 0:128] = strip_a[at, :].astype(BF16)
                 fsend[side, t * 2 + col, :, 128:256] = strip_b[at, :].astype(BF16)
 
@@ -153,11 +155,10 @@
     zero8 = jnp.zeros((8, 128), F32)
 
     def clear(r, _):
-        base = pl.multiple_of(r * FULL, 8)
-        uf[pl.ds(base, 8), :] = zero8
-        uf[pl.ds(base + 40, 8), :] = zero8
-        sf[pl.ds(base, 8), :] = zero8
-        sf[pl.ds(base + 40, 8), :] = zero8
+        uf[pl.ds(r * ODD_FULL, 8), :] = zero8
+        uf[pl.ds(r * ODD_FULL + 40, 8), :] = zero8
+        sf[pl.ds(r * ODD_FULL, 8), :] = zero8
+        sf[pl.ds(r * ODD_FULL + 40, 8), :] = zero8
         return 0
 
     lax.fori_loop(0, SLOTS * SIDE, clear, 0, unroll=8)
@@ -182,9 +183,9 @@
         for i in range(SIDE):
             r = t * SIDE + i
             rows = slice(i * SIDE, i * SIDE + SIDE)
-            y0[pl.ds(pl.multiple_of(r * WIDE + 8, 8), SIDE), :] = y[rows, 0:128]
-            y1[pl.ds(pl.multiple_of(r * SIDE, 8), SIDE), :] = y[rows, 128:256]
-            y2[pl.ds(pl.multiple_of(r * WIDE, 8), SIDE), :] = y[rows, 256:384]
+            y0[pl.ds(r * ODD_WIDE + 8, SIDE), :] = y[rows, 0:128]
+            y1[pl.ds(r * ODD_SIDE, SIDE), :] = y[rows, 128:256]
+            y2[pl.ds(r * ODD_WIDE, SIDE), :] = y[rows, 256:384]
         return 0
 
     lax.fori_loop(0, SLOTS, conv_mid, 0)
@@ -199,8 +200,8 @@
         for t in range(SLOTS):
             for col in range(2):
                 rows = slice((t * 2 + col) * 32, (t * 2 + col) * 32 + 32)
-                y0[pl.ds(t * SIDE * WIDE + 6 + col, SIDE, stride=WIDE), :] = west[rows]
-                y2[pl.ds(t * SIDE * WIDE + 32 + col, SIDE, stride=WIDE), :] = east[rows]
+                y0[pl.ds(t * SIDE * ODD_WIDE + 6 + col, SIDE, stride=ODD_WIDE), :] = west[rows]
+                y2[pl.ds(t * SIDE * ODD_WIDE + 32 + col, SIDE, stride=ODD_WIDE), :] = east[rows]
 
     add_margins(
         jnp.dot(sa_w[...], wmid[:, 0:128], preferred_element_type=F32),
@@ -210,9 +211,9 @@
     columns = ((0, 0, 0), (0, 1, 1), (1, 0, 30), (1, 1, 31))
 
     def mid_at(t, cell):
-        first = y0[pl.ds(t * SIDE * WIDE + 6 + cell, SIDE, stride=WIDE), :]
-        second = y1[pl.ds(t * CELLS + cell, SIDE, stride=SIDE), :]
-        third = y2[pl.ds(t * SIDE * WIDE + 2 + cell, SIDE, stride=WIDE), :]
+        first = y0[pl.ds(t * SIDE * ODD_WIDE + 6 + cell, SIDE, stride=ODD_WIDE), :]
+        second = y1[pl.ds(t * SIDE * ODD_SIDE + cell, SIDE, stride=ODD_SIDE), :]
+        third = y2[pl.ds(t * SIDE * ODD_WIDE + 2 + cell, SIDE, stride=ODD_WIDE), :]
         return first + second + third
 
     for t in range(SLOTS):
@@ -222,9 +223,9 @@
     hidden_copies = exchange(hsend, hrecv, 2)
 
     def mid_rows(r):
-        first = y0[pl.ds(r * WIDE + 6, SIDE), :]
-        second = y1[pl.ds(pl.multiple_of(r * SIDE, 8), SIDE), :]
-        third = y2[pl.ds(r * WIDE + 2, SIDE), :]
+        first = y0[pl.ds(r * ODD_WIDE + 6, SIDE), :]
+        second = y1[pl.ds(r * ODD_SIDE, SIDE), :]
+        third = y2[pl.ds(r * ODD_WIDE + 2, SIDE), :]
         return first + second + third
 
     def activate(r, _):
@@ -246,8 +247,8 @@
         for i in range(SIDE):
             r = t * SIDE + i
             rows = slice(i * SIDE, i * SIDE + SIDE)
-            ya[pl.ds(pl.multiple_of(r * FULL + 8, 8), SIDE), :] = y[rows, 0:128]
-            yb[pl.ds(pl.multiple_of(r * SIDE, 8), SIDE), :] = y[rows, 128:256]
+            ya[pl.ds(r * ODD_FULL + 8, SIDE), :] = y[rows, 0:128]
+            yb[pl.ds(r * ODD_SIDE, SIDE), :] = y[rows, 128:256]
         return 0
 
     lax.fori_loop(0, SLOTS, conv_top, 0)
@@ -261,17 +262,17 @@
     for t in range(SLOTS):
         for col in range(2):
             rows = slice((t * 2 + col) * 32, (t * 2 + col) * 32 + 32)
-            ya[pl.ds(t * SIDE * FULL + 6 + col, SIDE, stride=FULL), :] = west[rows]
-            ya[pl.ds(t * SIDE * FULL + 40 + col, SIDE, stride=FULL), :] = east[rows]
+            ya[pl.ds(t * SIDE * ODD_FULL + 6 + col, SIDE, stride=ODD_FULL), :] = west[rows]
+            ya[pl.ds(t * SIDE * ODD_FULL + 40 + col, SIDE, stride=ODD_FULL), :] = east[rows]
 
     zero_rows = jnp.zeros((SIDE, 128), F32)
 
     def up_pair(t, pair, mask):
         cell = 2 * pair
-        base = t * SIDE * FULL
-        before = [ya[pl.ds(base + 6 + cell + k, SIDE, stride=FULL), :] for k in range(2)]
-        after = [ya[pl.ds(base + 10 + cell + k, SIDE, stride=FULL), :] for k in range(2)]
-        centre = [yb[pl.ds(t * CELLS + cell + k, SIDE, stride=SIDE), :] for k in range(2)]
+        base = t * SIDE * ODD_FULL
+        before = [ya[pl.ds(base + 6 + cell + k, SIDE, stride=ODD_FULL), :] for k in range(2)]
+        after = [ya[pl.ds(base + 10 + cell + k, SIDE, stride=ODD_FULL), :] for k in range(2)]
+        centre = [yb[pl.ds(t * SIDE * ODD_SIDE + cell + k, SIDE, stride=ODD_SIDE), :] for k in range(2)]
         pre = jnp.where(low, before[0], after[1])
         pre = pre + pltpu.roll(jnp.where(low, before[1], after[0]), 64, 1)
         pre = pre + jnp.where(low, centre[0], centre[1]) + btop_twice
@@ -280,12 +281,12 @@
         lanes = pl.ds(pair * 128, 128)
         if not isinstance(pair, int):
             lanes = pl.ds(pl.multiple_of(pair * 128, 128), 128)
-        out[t, :, lanes] = (value * mask).astype(BF16)
+        outv[t, :, lanes] = (value * mask).astype(BF16)
         up = cotv[t, :, lanes].astype(F32) * (gate + value * (1.0 - gate)) * mask
         up = up.astype(BF16).astype(F32)
         turned = pltpu.roll(up, 64, 1)
-        uf[pl.ds(base + 8 + cell, SIDE, stride=FULL), :] = jnp.where(low, up, turned)
-        uf[pl.ds(base + 9 + cell, SIDE, stride=FULL), :] = jnp.where(low, turned, up)
+        uf[pl.ds(base + 8 + cell, SIDE, stride=ODD_FULL), :] = jnp.where(low, up, turned)
+        uf[pl.ds(base + 9 + cell, SIDE, stride=ODD_FULL), :] = jnp.where(low, turned, up)
         return up, turned
 
     def tile_sum(up):
@@ -309,6 +310,8 @@
         return total + tile_sum(up)
 
     bias_top = lax.fori_loop(0, SLOTS * 14, top_pairs, bias_top, unroll=7)
+    out_copy = pltpu.make_async_copy(outv, out, local_sem.at[14])
+    out_copy.start()
 
     def shift_up(g, _):
         at = pl.ds(pl.multiple_of(g * 128, 128), 128)
@@ -316,7 +319,7 @@
 
         def cells(first):
             return jnp.concatenate(
-                [uf[pl.ds((g * 4 + k) * FULL + first, SIDE), :] for k in range(4)], axis=0)
+                [uf[pl.ds((g * 4 + k) * ODD_FULL + first, SIDE), :] for k in range(4)], axis=0)
 
         left_half = low_lanes((128, 128))
         zero = jnp.zeros((128, 128), F32)
@@ -341,13 +344,10 @@
     edges = lax.dot_general(edges_l, edges_r, across, preferred_element_type=F32)
     acc_top[...] = edges[0:192]
 
-    def grad_top(t, _):
+    def grad_top(t):
         rhs = jnp.concatenate([hp[t, 64 * a : 64 * a + CELLS, :] for a in range(3)], axis=1)
         lhs = uut[:, pl.ds(pl.multiple_of(t * CELLS, 128), CELLS)]
         acc_top[...] += jnp.dot(lhs, rhs, preferred_element_type=F32)
-        return 0
-
-    lax.fori_loop(0, SLOTS, grad_top, 0)
 
     def conv_back(t, _):
         first = uplo[t, 0:CELLS, :] + uphi[t, 64 : 64 + CELLS, :]
@@ -356,9 +356,9 @@
         for i in range(SIDE):
             r = t * SIDE + i
             rows = slice(i * SIDE, i * SIDE + SIDE)
-            y0[pl.ds(pl.multiple_of(r * WIDE + 8, 8), SIDE), :] = y[rows, 0:128]
-            y1[pl.ds(pl.multiple_of(r * SIDE, 8), SIDE), :] = y[rows, 128:256]
-            y2[pl.ds(pl.multiple_of(r * WIDE, 8), SIDE), :] = y[rows, 256:384]
+            y0[pl.ds(r * ODD_WIDE + 8, SIDE), :] = y[rows, 0:128]
+            y1[pl.ds(r * ODD_SIDE, SIDE), :] = y[rows, 128:256]
+            y2[pl.ds(r * ODD_WIDE, SIDE), :] = y[rows, 256:384]
         return 0
 
     lax.fori_loop(0, SLOTS, conv_back, 0)
@@ -387,29 +387,49 @@
         jnp.dot(su_w[...], wback[:, 0:128], preferred_element_type=F32),
         jnp.dot(su_e[...], wback[:, 256:384], preferred_element_type=F32))
 
-    def slopes(r, total):
-        back = mid_rows(r) * slope[pl.ds(pl.multiple_of(r * SIDE, 8), SIDE), :]
-        back = back.astype(BF16).astype(F32)
-        sf[pl.ds(pl.multiple_of(r * FULL + 8, 8), SIDE), :] = back
-        return total + jnp.sum(back.reshape(4, 8, 128), axis=0)
-
-    bias_mid = lax.fori_loop(0, SLOTS * SIDE, slopes, jnp.zeros((8, 128), F32), unroll=4)
-
-    def shift_slope(g, _):
-        at = pl.ds(pl.multiple_of(g * 128, 128), 128)
-        for b, first in enumerate((10, 8, 6)):
-            rows = [sf[pl.ds((g * 4 + k) * FULL + first, SIDE), :] for k in range(4)]
-            block = jnp.concatenate(rows, axis=0).astype(BF16)
-            sst[b * 128 : b * 128 + 128, at] = block.T
-        return 0
-
-    lax.fori_loop(0, SLOTS * SIDE // 4, shift_slope, 0, unroll=4)
+    def slopes(t, total):
+        for i in range(SIDE):
+            r = t * SIDE + i
+            back = mid_rows(r) * slope[pl.ds(pl.multiple_of(r * SIDE, 8), SIDE), :]
+            back = back.astype(BF16).astype(F32)
+            sf[pl.ds(r * ODD_FULL + 8, SIDE), :] = back
+            total = total + tile_sum(back)
+        return total
+
+    def turn_slopes(t):
+        for quarter in range(8):
+            g = t * 8 + quarter
+            at = pl.ds(pl.multiple_of(g * 128, 128), 128)
+            for b, first in enumerate((10, 8, 6)):
+                rows = [sf[pl.ds((g * 4 + k) * ODD_FULL + first, SIDE), :] for k in range(4)]
+                block = jnp.concatenate(rows, axis=0).astype(BF16)
+                sst[b * 128 : b * 128 + 128, at] = block.T
+
+    bias_mid = slopes(0, jnp.zeros((8, 128), F32))
+    grad_top(0)
+
+    def slopes_and_turn(t, total):
+        turn_slopes(t - 1)
+        grad_top(t)
+        return slopes(t, total)
+
+    bias_mid = lax.fori_loop(1, SLOTS, slopes_and_turn, bias_mid)
+    turn_slopes(SLOTS - 1)
     for t in range(SLOTS):
         for side, col, cell in columns:
             edge = scol_w if side == 0 else scol_e
             at = (t * 2 + col) * 32
             edge[at : at + 32, :] = sf[
-                pl.ds(t * SIDE * FULL + 8 + cell, SIDE, stride=FULL), :].astype(BF16)
+                pl.ds(t * SIDE * ODD_FULL + 8 + cell, SIDE, stride=ODD_FULL), :].astype(BF16)
+
+    def in_halves(value):
+        rounded = value.astype(BF16).astype(F32)
+        return jnp.concatenate([rounded, value - rounded], axis=0)
+
+    def split_again(rows, here):
+        split = in_halves(rows[0:16] + rows[16:32])
+        chosen = jnp.where(here, 1.0, 0.0).astype(F32)
+        return split * chosen + rows * (1.0 - chosen)
 
     def reducer(chunk, order):
         base = chunk * 1024
@@ -435,13 +455,15 @@
             return pl.ds(pl.multiple_of(offset + index * size, 16), size)
 
         def split_core():
-            sum_core[chunk] = grad[base : base + 1024, :].astype(BF16)
-            send(0, sum_core.at[chunk, rows_at(1 - core, 512)], core_in.at[chunk], other)
+            send(0, grad.at[rows_at(1 - core, 512, base)], core_in.at[chunk], other)
 
         def split_plane():
             arrive()
-            mine = grad[rows_at(core, 512, base), :]
-            plane_out[chunk] = (mine + core_in[chunk].astype(F32)).astype(BF16)
+            mine = grad[rows_at(core, 512, base), :].astype(F32)
+            value = mine + core_in[chunk].astype(F32)
+            plane_out[chunk] = value.astype(BF16)
+            if chunk == 0:
+                plane_out[chunk, 64:96] = split_again(value[64:96], core == 1).astype(BF16)
             for k, (d, e) in enumerate(corners):
                 there = moved(((first, d), (second, e)))
                 to = there[first] * 4 + there[second]
@@ -463,6 +485,8 @@
             arrive()
             value = line_in[chunk, 0] + line_in[chunk, 1]
             value = value + (line_in[chunk, 2] + line_in[chunk, 3])
+            if chunk == 0:
+                value = split_again(value, core * 16 + shard == 18)
             mine = rows_at(core * 16 + shard, 32, base)
             total[mine, :] = value.astype(BF16)
             for k, (d, e) in enumerate(corners):
@@ -476,8 +500,12 @@
 
         def finish():
             arrive()
+            whole = pltpu.make_async_copy(
+                total.at[pl.ds(base, 1024)], sums.at[pl.ds(base, 1024)], local_sem.at[15 + chunk])
+            whole.start()
             for copy in started:
                 copy.wait_send()
+            whole.wait()
 
         return iter((split_core, split_plane, swap_line, back_plane, back_core, finish))
 
@@ -492,58 +520,64 @@
     for a in range(3):
         for b in range(3):
             at = (a * 3 + b) * 64
-            grad[at : at + 64, :] = acc_top[b * 64 : b * 64 + 64, a * 128 : a * 128 + 128]
-    grad[576:584, :] = bias_mid
-    grad[584:592, :] = bias_top
-    grad[592:768, :] = jnp.zeros((176, 128), F32)
+            block = acc_top[b * 64 : b * 64 + 64, a * 128 : a * 128 + 128]
+            grad[at : at + 64, :] = block.astype(BF16)
+    grad[576:608, :] = in_halves(jnp.concatenate([bias_mid, bias_top], axis=0)).astype(BF16)
+    grad[608:768, :] = jnp.zeros((160, 128), BF16)
 
     for a in range(3):
         q = slice(a * 256, a * 256 + 256)
-        acc_mid[0:128, :] = lax.dot_general(
-            scol_w[...], sa_w[:, q], across, preferred_element_type=F32)
-        acc_mid[128:256, :] = jnp.zeros((128, 256), F32)
-        acc_mid[256:384, :] = lax.dot_general(
-            scol_e[...], sa_e[:, q], across, preferred_element_type=F32)
-
-        def grad_mid(t, _):
-            acc_mid[...] += jnp.dot(
-                sst[:, pl.ds(pl.multiple_of(t * CELLS, 128), CELLS)],
-                fp[t, 64 * a : 64 * a + CELLS, :], preferred_element_type=F32)
-            return 0
-
-        lax.fori_loop(0, SLOTS, grad_mid, 0)
-        for b in range(3):
+        rhs = jnp.concatenate(
+            [fp[t, 64 * a : 64 * a + CELLS, :] for t in range(SLOTS)], axis=0)
+        acc = jnp.dot(sst[...], rhs, preferred_element_type=F32)
+        west = lax.dot_general(scol_w[...], sa_w[:, q], across, preferred_element_type=F32)
+        east = lax.dot_general(scol_e[...], sa_e[:, q], across, preferred_element_type=F32)
+        for b, block in enumerate((acc[0:128] + west, acc[128:256], acc[256:384] + east)):
             at = 768 + (a * 3 + b) * 256
-            grad[at : at + 256, :] = acc_mid[b * 128 : b * 128 + 128, :].T
+            grad[at : at + 256, :] = block.astype(BF16).T
         advance(*((0,), (1, 0), (2, 1, 2))[a])
     for _ in range(4):
         advance(0, 1, 2)
 
-    sums[...] = total[...]
-
-
-def finish_kernel(sums, out_in, gmid, gtop, bmid, btop, out, mid_half, mid_full, top_half, out_held, sem):
-    whole = pltpu.make_async_copy(out_in, out_held, sem.at[0])
-    top = pltpu.make_async_copy(sums.at[pl.ds(0, 592)], top_half, sem.at[1])
-    mid = pltpu.make_async_copy(sums.at[pl.ds(768, 2304)], mid_half, sem.at[2])
-    mid.start()
-    whole.start()
-    top.start()
-    mid.wait()
-    mid_full[...] = mid_half[...].astype(F32)
-    mid_back = pltpu.make_async_copy(mid_full, gmid, sem.at[3])
-    mid_back.start()
-    whole.wait()
-    whole_back = pltpu.make_async_copy(out_held, out, sem.at[4])
-    whole_back.start()
+    out_copy.wait()
+
+
+def finish_kernel(
+    sums, out_in, gmid, gtop, bmid, btop, out,
+    mid_half, mid_full, top_half, top_full, bmid_full, btop_full, out_held, sem,
+):
+    mids, backs = [], []
+    for k in range(3):
+        rows = pl.ds(k * 768, 768)
+        mids.append(pltpu.make_async_copy(
+            sums.at[pl.ds(768 + k * 768, 768)], mid_half.at[rows], sem.at[k]))
+        backs.append(pltpu.make_async_copy(mid_full.at[rows], gmid.at[rows], sem.at[3 + k]))
+    top = pltpu.make_async_copy(sums.at[pl.ds(0, 608)], top_half, sem.at[6])
+    held = pltpu.make_async_copy(out_in, out_held, sem.at[7])
+    top_back = pltpu.make_async_copy(top_full, gtop, sem.at[8])
+    held_back = pltpu.make_async_copy(out_held, out, sem.at[9])
+    bmid_back = pltpu.make_async_copy(bmid_full, bmid, sem.at[10])
+    btop_back = pltpu.make_async_copy(btop_full, btop, sem.at[11])
+    for copy in (top, *mids, held):
+        copy.start()
     top.wait()
-    gtop[...] = top_half[0:576, :].astype(F32)
-    tail = top_half[576:592, :].astype(F32)
-    bmid[...] = jnp.sum(tail[0:8], axis=0, keepdims=True)
+    top_full[...] = top_half[0:576, :].astype(F32)
+    top_back.start()
+    tail = top_half[576:592, :].astype(F32) + top_half[592:608, :].astype(F32)
+    bmid_full[...] = jnp.sum(tail[0:8], axis=0, keepdims=True)
+    bmid_back.start()
     twice = jnp.sum(tail[8:16], axis=0, keepdims=True)
-    btop[...] = twice[:, 0:64] + twice[:, 64:128]
-    mid_back.wait()
-    whole_back.wait()
+    btop_full[...] = twice[:, 0:64] + twice[:, 64:128]
+    btop_back.start()
+    for k in range(3):
+        mids[k].wait()
+        rows = slice(k * 768, k * 768 + 768)
+        mid_full[rows, :] = mid_half[rows, :].astype(F32)
+        backs[k].start()
+    held.wait()
+    held_back.start()
+    for copy in (top_back, bmid_back, btop_back, *backs, held_back):
+        copy.wait()
 
 
 def shards(features, cotangent, neighbors, live_count, kernel_mid, bias_mid, kernel_top, bias_top):
@@ -559,18 +593,18 @@
             jax.ShapeDtypeStruct((3072, 128), BF16),
         ),
         in_specs=[hbm, hbm, smem, smem, hbm, vmem, vmem, vmem],
-        out_specs=(vmem, vmem),
+        out_specs=(hbm, hbm),
         scratch_shapes=[
             pltpu.VMEM((SLOTS, PADDED, 256), BF16),
             pltpu.VMEM((SLOTS, PADDED, 128), BF16),
             pltpu.VMEM((768, 384), BF16),
             pltpu.VMEM((384, 256), BF16),
             pltpu.VMEM((256, 384), BF16),
-            pltpu.VMEM((rows * WIDE, 128), F32),
-            pltpu.VMEM((rows * SIDE, 128), F32),
-            pltpu.VMEM((rows * WIDE, 128), F32),
-            pltpu.VMEM((rows * FULL, 128), F32),
-            pltpu.VMEM((rows * SIDE, 128), F32),
+            pltpu.VMEM((rows * ODD_WIDE, 128), F32),
+            pltpu.VMEM((rows * ODD_SIDE, 128), F32),
+            pltpu.VMEM((rows * ODD_WIDE, 128), F32),
+            pltpu.VMEM((rows * ODD_FULL, 128), F32),
+            pltpu.VMEM((rows * ODD_SIDE, 128), F32),
             pltpu.VMEM((8 * FULL, 128), F32),
             pltpu.VMEM((256, 768), BF16),
             pltpu.VMEM((256, 768), BF16),
@@ -578,8 +612,8 @@
             pltpu.VMEM((256, 384), BF16),
             pltpu.VMEM((256, 256), BF16),
             pltpu.VMEM((256, 256), BF16),
-            pltpu.VMEM((rows * 8, 128), F32),
-            pltpu.VMEM((rows * 8, 128), F32),
+            pltpu.VMEM((rows * 9, 128), F32),
+            pltpu.VMEM((rows * 9, 128), F32),
             pltpu.VMEM((2, 8, 32, 256), BF16),
             pltpu.VMEM((2, 8, 32, 256), BF16),
             pltpu.VMEM((2, 8, 32, 128), BF16),
@@ -587,7 +621,7 @@
             pltpu.VMEM((2, 4, 32, 128), BF16),
             pltpu.VMEM((2, 4, 32, 128), BF16),
             pltpu.VMEM((rows * SIDE, 128), F32),
-            pltpu.VMEM((rows * FULL, 128), F32),
+            pltpu.VMEM((rows * ODD_FULL, 128), F32),
             pltpu.VMEM((SLOTS, PADDED, 128), BF16),
             pltpu.VMEM((SLOTS, PADDED, 128), BF16),
             pltpu.VMEM((192, rows * SIDE), BF16),
@@ -595,19 +629,18 @@
             pltpu.VMEM((256, 128), BF16),
             pltpu.VMEM((256, 128), BF16),
             pltpu.VMEM((256, 128), BF16),
-            pltpu.VMEM((rows * FULL, 128), F32),
+            pltpu.VMEM((rows * ODD_FULL, 128), F32),
             pltpu.VMEM((384, rows * SIDE), BF16),
-            pltpu.VMEM((384, 256), F32),
             pltpu.VMEM((192, 384), F32),
             pltpu.VMEM((SLOTS, SIDE, 2048), BF16),
-            pltpu.VMEM((3072, 128), F32),
-            pltpu.VMEM((3, 1024, 128), BF16),
+            pltpu.VMEM((SLOTS, SIDE, 2048), BF16),
+            pltpu.VMEM((3072, 128), BF16),
             pltpu.VMEM((3, 512, 128), BF16),
             pltpu.VMEM((3, 512, 128), BF16),
             pltpu.VMEM((3, 15, 32, 128), BF16),
             pltpu.VMEM((3, 4, 32, 128), F32),
             pltpu.VMEM((3072, 128), BF16),
-            pltpu.SemaphoreType.DMA((14,)),
+            pltpu.SemaphoreType.DMA((18,)),
             pltpu.SemaphoreType.DMA((6,)),
             pltpu.SemaphoreType.DMA((6,)),
             pltpu.SemaphoreType.DMA((3, 35)),
@@ -631,13 +664,16 @@
             jax.ShapeDtypeStruct((SLOTS, SIDE, 2048), BF16),
         ),
         in_specs=[hbm, hbm],
-        out_specs=(hbm, vmem, vmem, vmem, hbm),
+        out_specs=(hbm,) * 5,
         scratch_shapes=[
             pltpu.VMEM((2304, 128), BF16),
             pltpu.VMEM((2304, 128), F32),
-            pltpu.VMEM((592, 128), BF16),
+            pltpu.VMEM((608, 128), BF16),
+            pltpu.VMEM((576, 128), F32),
+            pltpu.VMEM((1, 128), F32),
+            pltpu.VMEM((1, 64), F32),
             pltpu.VMEM((SLOTS, SIDE, 2048), BF16),
-            pltpu.SemaphoreType.DMA((5,)),
+            pltpu.SemaphoreType.DMA((12,)),
         ],
         compiler_params=pltpu.CompilerParams(vmem_limit_bytes=60 * 2**20),
         name="finish",

time: 60.1 us -> 54.7 us (0.910)
  Pallas kernels: 58.6 us -> 53.2 us
    pallas_call x1, Pallas kernels: 55.5 us -> 50.9 us  [shards(): pl.pallas_call(kernel, out_shape=(jax.ShapeDtypeStruct((SLOTS, SIDE, 2048...]
    pallas_call x1, Pallas kernels: 3.09 us -> 2.33 us  [shards(): pl.pallas_call(finish_kernel, out_shape=(jax.ShapeDtypeStruct((2304, 128)...]
where the time goes in v3:
time: 54.7 us; the launch traced here: 54.5 us
  Pallas kernels  53.2 us (97%)
  between operations  1.29 us (2%)
    pallas_call x1, Pallas kernels, shards(): pl.pallas_call(kernel, out_shape=(jax.ShapeDtypeStruct((SLOTS, SIDE, 2048...  50.9 us
    pallas_call x1, Pallas kernels, shards(): pl.pallas_call(finish_kernel, out_shape=(jax.ShapeDtypeStruct((2304, 128)...  2.33 us

profile of v3, /device:TPU:1, one launch (start us, length us, event | category | flops | bytes accessed | tf_op | source)
XLA Modules:
  0.0 54.5 jit_solution(9946032631645691551)
XLA Ops:
  1.3 50.9 %backend_layers.1 = (bf16[4,32,2048]{2,1,0:T(8,128)(2,1)}, bf16[3072,128]{1,0:T(8,128)(2,1)}) custom-call(bf16[4,1024,256]{2,1,0:T(8,128)(2,1)} %bitcast.10, bf16[4,32,2048]{2,1,0:T(8,128)(2,1)} %cot.1, s32[4,8]{1,0:T(4,128)} %nbr.1, s32[1]{0:T(128)S(6)} %copy.13.live, bf16[3,3,256,128]{3,2,1,0:T(8,128)(2,1)} %kmid.1, f32[1,128]{1,0:T(1,128)} %bitcast.12, ...), custom_call_target="tpu_custom_call" | custom-call | tf_op jit(solution)/shard_map/backend_layers/pallas_call | solution.py:589
  52.2 2.3 %finish.1 = (f32[2304,128]{1,0:T(8,128)}, f32[576,128]{1,0:T(8,128)}, f32[1,128]{1,0:T(1,128)}, f32[1,64]{1,0:T(1,128)}, bf16[4,32,2048]{2,1,0:T(8,128)(2,1)}) custom-call(bf16[3072,128]{1,0:T(8,128)(2,1)} %get-tuple-element.12.sums, bf16[4,32,2048]{2,1,0:T(8,128)(2,1)} %get-tuple-element.13.out_in), custom_call_target="tpu_custom_call" | custom-call | tf_op jit(solution)/shard_map/finish/pallas_call | solution.py:657

commit v4 on v3

--- a/solution.py
+++ b/solution.py
@@ -238,7 +238,7 @@
         slope[pl.ds(pl.multiple_of(r * SIDE, 8), SIDE), :] = (gate + hidden * (1.0 - gate)) * mask
         return 0
 
-    lax.fori_loop(0, SLOTS * SIDE, activate, 0, unroll=4)
+    lax.fori_loop(0, SLOTS * SIDE, activate, 0, unroll=8)
     fill_bands(hp, nbr)
 
     def conv_top(t, _):
@@ -251,7 +251,7 @@
             yb[pl.ds(r * ODD_SIDE, SIDE), :] = y[rows, 128:256]
         return 0
 
-    lax.fori_loop(0, SLOTS, conv_top, 0)
+    lax.fori_loop(0, SLOTS, conv_top, 0, unroll=2)
 
     for copy in hidden_copies:
         copy.wait()
@@ -309,7 +309,7 @@
         up, _ = up_pair(t, pair, mask)
         return total + tile_sum(up)
 
-    bias_top = lax.fori_loop(0, SLOTS * 14, top_pairs, bias_top, unroll=7)
+    bias_top = lax.fori_loop(0, SLOTS * 14, top_pairs, bias_top, unroll=14)
     out_copy = pltpu.make_async_copy(outv, out, local_sem.at[14])
     out_copy.start()
 
@@ -331,7 +331,7 @@
         uut[128:192, at] = cells(6).astype(BF16).T[0:64]
         return 0
 
-    lax.fori_loop(0, SLOTS * SIDE // 4, shift_up, 0, unroll=4)
+    lax.fori_loop(0, SLOTS * SIDE // 4, shift_up, 0, unroll=8)
     fill_bands(uplo, nbr)
     fill_bands(uphi, nbr)
 
@@ -361,7 +361,7 @@
             y2[pl.ds(r * ODD_WIDE, SIDE), :] = y[rows, 256:384]
         return 0
 
-    lax.fori_loop(0, SLOTS, conv_back, 0)
+    lax.fori_loop(0, SLOTS, conv_back, 0, unroll=2)
 
     for copy in upstream_copies:
         copy.wait()
@@ -503,11 +503,15 @@
             whole = pltpu.make_async_copy(
                 total.at[pl.ds(base, 1024)], sums.at[pl.ds(base, 1024)], local_sem.at[15 + chunk])
             whole.start()
-            for copy in started:
+            started.append(whole)
+
+        def drain():
+            *sent, whole = started
+            for copy in sent:
                 copy.wait_send()
             whole.wait()
 
-        return iter((split_core, split_plane, swap_line, back_plane, back_core, finish))
+        return iter((split_core, split_plane, swap_line, back_plane, back_core, finish, drain))
 
     reducers = [reducer(chunk, order) for chunk, order in enumerate(orders)]
 
@@ -536,7 +540,7 @@
             at = 768 + (a * 3 + b) * 256
             grad[at : at + 256, :] = block.astype(BF16).T
         advance(*((0,), (1, 0), (2, 1, 2))[a])
-    for _ in range(4):
+    for _ in range(5):
         advance(0, 1, 2)
 
     out_copy.wait()

time: 54.7 us -> 53.8 us (0.984)
  Pallas kernels: 53.2 us -> 52.4 us
    pallas_call x1, Pallas kernels: 50.9 us -> 50 us  [shards(): pl.pallas_call(kernel, out_shape=(jax.ShapeDtypeStruct((SLOTS, SIDE, 2048...]
where the time goes in v4:
time: 53.8 us; the launch traced here: 53.7 us
  Pallas kernels  52.4 us (97%)
  between operations  1.29 us (2%)
    pallas_call x1, Pallas kernels, shards(): pl.pallas_call(kernel, out_shape=(jax.ShapeDtypeStruct((SLOTS, SIDE, 2048...  50 us
    pallas_call x1, Pallas kernels, shards(): pl.pallas_call(finish_kernel, out_shape=(jax.ShapeDtypeStruct((2304, 128)...  2.33 us

profile of v4, /device:TPU:1, one launch (start us, length us, event | category | flops | bytes accessed | tf_op | source)
XLA Modules:
  0.0 53.7 jit_solution(9822600179826644092)
XLA Ops:
  1.3 50.0 %backend_layers.1 = (bf16[4,32,2048]{2,1,0:T(8,128)(2,1)}, bf16[3072,128]{1,0:T(8,128)(2,1)}) custom-call(bf16[4,1024,256]{2,1,0:T(8,128)(2,1)} %bitcast.10, bf16[4,32,2048]{2,1,0:T(8,128)(2,1)} %cot.1, s32[4,8]{1,0:T(4,128)} %nbr.1, s32[1]{0:T(128)S(6)} %copy.13.live, bf16[3,3,256,128]{3,2,1,0:T(8,128)(2,1)} %kmid.1, f32[1,128]{1,0:T(1,128)} %bitcast.12, ...), custom_call_target="tpu_custom_call" | custom-call | tf_op jit(solution)/shard_map/backend_layers/pallas_call | solution.py:593
  51.3 2.3 %finish.1 = (f32[2304,128]{1,0:T(8,128)}, f32[576,128]{1,0:T(8,128)}, f32[1,128]{1,0:T(1,128)}, f32[1,64]{1,0:T(1,128)}, bf16[4,32,2048]{2,1,0:T(8,128)(2,1)}) custom-call(bf16[3072,128]{1,0:T(8,128)(2,1)} %get-tuple-element.12.sums, bf16[4,32,2048]{2,1,0:T(8,128)(2,1)} %get-tuple-element.13.out_in), custom_call_target="tpu_custom_call" | custom-call | tf_op jit(solution)/shard_map/finish/pallas_call | solution.py:661

commit v5 on v4

--- a/solution.py
+++ b/solution.py
@@ -536,10 +536,13 @@
         acc = jnp.dot(sst[...], rhs, preferred_element_type=F32)
         west = lax.dot_general(scol_w[...], sa_w[:, q], across, preferred_element_type=F32)
         east = lax.dot_general(scol_e[...], sa_e[:, q], across, preferred_element_type=F32)
+        if a:
+            advance(a - 1)
         for b, block in enumerate((acc[0:128] + west, acc[128:256], acc[256:384] + east)):
             at = 768 + (a * 3 + b) * 256
             grad[at : at + 256, :] = block.astype(BF16).T
-        advance(*((0,), (1, 0), (2, 1, 2))[a])
+        advance(a)
+    advance(2)
     for _ in range(5):
         advance(0, 1, 2)
 

time: 53.8 us -> 54.1 us (level)
  no operation moved by 1% of the time
where the time goes in v5:
time: 54.1 us; the launch traced here: 53.9 us
  Pallas kernels  52.6 us (97%)
  between operations  1.29 us (2%)
    pallas_call x1, Pallas kernels, shards(): pl.pallas_call(kernel, out_shape=(jax.ShapeDtypeStruct((SLOTS, SIDE, 2048...  50.3 us
    pallas_call x1, Pallas kernels, shards(): pl.pallas_call(finish_kernel, out_shape=(jax.ShapeDtypeStruct((2304, 128)...  2.33 us

profile of v5, /device:TPU:1, one launch (start us, length us, event | category | flops | bytes accessed | tf_op | source)
XLA Modules:
  0.0 53.9 jit_solution(6889282028252485153)
XLA Ops:
  1.3 50.3 %backend_layers.1 = (bf16[4,32,2048]{2,1,0:T(8,128)(2,1)}, bf16[3072,128]{1,0:T(8,128)(2,1)}) custom-call(bf16[4,1024,256]{2,1,0:T(8,128)(2,1)} %bitcast.10, bf16[4,32,2048]{2,1,0:T(8,128)(2,1)} %cot.1, s32[4,8]{1,0:T(4,128)} %nbr.1, s32[1]{0:T(128)S(6)} %copy.13.live, bf16[3,3,256,128]{3,2,1,0:T(8,128)(2,1)} %kmid.1, f32[1,128]{1,0:T(1,128)} %bitcast.12, ...), custom_call_target="tpu_custom_call" | custom-call | tf_op jit(solution)/shard_map/backend_layers/pallas_call | solution.py:596
  51.6 2.3 %finish.1 = (f32[2304,128]{1,0:T(8,128)}, f32[576,128]{1,0:T(8,128)}, f32[1,128]{1,0:T(1,128)}, f32[1,64]{1,0:T(1,128)}, bf16[4,32,2048]{2,1,0:T(8,128)(2,1)}) custom-call(bf16[3072,128]{1,0:T(8,128)(2,1)} %get-tuple-element.12.sums, bf16[4,32,2048]{2,1,0:T(8,128)(2,1)} %get-tuple-element.13.out_in), custom_call_target="tpu_custom_call" | custom-call | tf_op jit(solution)/shard_map/finish/pallas_call | solution.py:664
